TPU v7x, 256 devices: a whole 4x4x8 slice. The times are simulated.
256 devices in a mesh: group: 8 (over z), dom: 32 (over y, x, core).
Axes of the slice: x: 4, y: 4, z: 8, core: 2. Of those that a mesh axis runs over, the one named last changes fastest.
Arguments:
- positions: float32 [3, 8388608], P(None, ('group', 'dom')), may hold values from -1 to 1
- masses: float32 [8388608], P(('group', 'dom')), may hold values from 0.002 to 0.02
- near_target: int32 [1048576], P(('group', 'dom')), may hold values from 0 to 511
- near_source: int32 [1048576], P(('group', 'dom')), may hold values from 0 to 515
- near_count: int32 [256], P(('group', 'dom')), may hold values from 1024 to 4096, as said below
- far_target: int32 [4194304], P(('group', 'dom')), may hold values from 0 to 511
- far_source: int32 [4194304], P(('group', 'dom')), may hold values from 0 to 2047, as said below
- far_class: int32 [32768], P(('group', 'dom')), may hold values from 0 to 315
- far_count: int32 [32768], P(('group', 'dom')), may hold values from 1 to 128, as said below
- export_slots: int32 [65536, 8], P(('group', 'dom')), may hold values from 0 to 511
- operators: float32 [316, 7056], replicated, may hold values from -0.625 to 0.625
Outputs:
- potential: float32 [8388608], P(('group', 'dom'))
Inputs may be any that keep to these rules, and one draw needn't show every extreme that they name: Pairs at positions near_count and later of a device's list are padding; some device's list is full. `far_count`: live pairs stand first in their batch; some batch is full. `far_source`: the slot of device s holding export slot c is s * 8 + c.
All inputs are finite; a program needn't handle non-finite values.
Results may differ from a plain program's by a relative error of at most 0.0003.
Values sent between devices are 32-bit elements; how exact they have to be, the bound alone decides.
A program may use at most 192 MiB of HBM per device.

v0:
```python
import math

import jax
import jax.numpy as jnp
import numpy as np
from jax import lax
from jax.sharding import PartitionSpec as P

LEAF_SIZE = 64
ORDER = 6
RIM = 2


softening = 0.01


def padded(cells, sides, width):
    for axis, dim in sides:
        count = lax.axis_size(axis)
        ends = count - 1
        head = lax.slice_in_dim(cells, 0, width, axis=dim)
        tail = lax.slice_in_dim(cells, cells.shape[dim] - width, cells.shape[dim], axis=dim)
        cells = jnp.concatenate(
            [
                lax.ppermute(tail, axis, [(i, (i + 1) % count) for i in range(ends)]),
                cells,
                lax.ppermute(head, axis, [((i + 1) % count, i) for i in range(ends)]),
            ],
            axis=dim,
        )
    return cells


def exponent_table(degree_max):
    triples = []
    for degree in range(degree_max + 1):
        for first_pow in range(degree, -1, -1):
            for second_pow in range(degree - first_pow, -1, -1):
                triples.append((first_pow, second_pow, degree - first_pow - second_pow))
    return triples


def parity_signs(degree_max):
    return np.array(
        [(-1.0) ** (triple[0] + triple[1] + triple[2]) for triple in exponent_table(degree_max)],
        dtype=np.float32,
    )


def monomials(relative, degree_max):
    powers = []
    for axis_index in range(3):
        column = [jnp.ones_like(relative[axis_index])]
        for power_step in range(degree_max):
            column.append(column[-1] * relative[axis_index])
        powers.append(column)
    return jnp.stack(
        [
            powers[0][triple[0]] * powers[1][triple[1]] * powers[2][triple[2]]
            for triple in exponent_table(degree_max)
        ],
        axis=0,
    )


def leaf_terms(positions, masses, leaf_size):
    leaf_count = positions.shape[1] // leaf_size
    placed = positions.reshape(3, leaf_count, leaf_size)
    centre = jnp.mean(placed, axis=2, keepdims=True)
    monomial = monomials(placed - centre, ORDER)
    multipole = jnp.sum(monomial * masses.reshape(1, leaf_count, leaf_size), axis=2)
    return (monomial, multipole)


def far_terms(multipole, received, far_target, far_source, far_class, far_count, operators):
    coeffs = multipole.shape[0]
    batches = far_class.shape[0]
    batch_size = far_target.shape[0] // batches
    operator = operators[far_class].reshape(batches, coeffs, coeffs)
    usable = (jnp.arange(batch_size, dtype=jnp.int32)[None, :] < far_count[:, None]).astype(
        jnp.float32
    )[:, :, None]
    source_rows = received[far_source].reshape(batches, batch_size, coeffs)
    target_rows = multipole.T[far_target].reshape(batches, batch_size, coeffs)
    parity_sign = jnp.asarray(parity_signs(ORDER), dtype=jnp.float32)
    to_target = (
        jnp.einsum("nkj,nbj->nbk", operator, source_rows, precision=lax.Precision.HIGHEST) * usable
    )
    to_source = (
        parity_sign
        * jnp.einsum(
            "nkj,nbj->nbk", operator, target_rows * parity_sign, precision=lax.Precision.HIGHEST
        )
        * usable
    )
    local_part = (
        jnp.zeros((multipole.shape[1], coeffs), jnp.float32)
        .at[far_target]
        .add(to_target.reshape(-1, coeffs))
    )
    reaction = (
        jnp.zeros((received.shape[0], coeffs), jnp.float32)
        .at[far_source]
        .add(to_source.reshape(-1, coeffs))
    )
    return (local_part, reaction)


def near_field(own_leaves, ext_leaves, near_target, near_source, live_count):
    pair_count = near_target.shape[0]
    block_size = math.gcd(pair_count, 256)
    block_count = pair_count // block_size
    order_ids = jnp.arange(pair_count, dtype=jnp.int32).reshape(block_count, block_size)

    def one_block(totals, inputs):
        target_ids, source_ids, position_ids = inputs
        target_leaf = own_leaves[target_ids]
        source_leaf = ext_leaves[source_ids]
        offsets = target_leaf[:, :3, :, None] - source_leaf[:, :3, None, :]
        distance = jnp.sum(offsets * offsets, axis=1)
        inverse = jnp.where(distance > 0.0, lax.rsqrt(distance + softening), 0.0)
        potential_part = -jnp.sum(inverse * source_leaf[:, 3, None, :], axis=2)
        potential_part = potential_part * (position_ids < live_count).astype(jnp.float32)[:, None]
        return (totals.at[target_ids].add(potential_part), None)

    starting = jnp.zeros((own_leaves.shape[0], own_leaves.shape[2]), jnp.float32)
    inputs = (
        near_target.reshape(block_count, block_size),
        near_source.reshape(block_count, block_size),
        order_ids,
    )
    return lax.scan(one_block, starting, inputs)[0]


def local(
    positions,
    masses,
    near_target,
    near_source,
    near_count,
    far_target,
    far_source,
    far_class,
    far_count,
    export_slots,
    operators,
):
    groups = lax.axis_size("group")
    domains = lax.axis_size("dom")
    devices = groups * domains
    leaves = masses.shape[0] // LEAF_SIZE
    slot_count = export_slots.shape[1]
    monomial, multipole = leaf_terms(positions, masses, LEAF_SIZE)
    coeffs = multipole.shape[0]
    export_flat = export_slots.reshape(-1)
    outgoing = multipole[:, export_flat].T.reshape(groups, domains, slot_count * coeffs)
    incoming = lax.all_to_all(
        lax.all_to_all(outgoing, "group", split_axis=0, concat_axis=0, tiled=True),
        "dom",
        split_axis=1,
        concat_axis=1,
        tiled=True,
    )
    received = incoming.reshape(devices * slot_count, coeffs)
    local_part, reaction = far_terms(
        multipole, received, far_target, far_source, far_class, far_count, operators
    )
    packed = reaction.reshape(groups, domains, slot_count * coeffs)
    returned = lax.all_to_all(
        lax.all_to_all(packed, "group", split_axis=0, concat_axis=0, tiled=True),
        "dom",
        split_axis=1,
        concat_axis=1,
        tiled=True,
    )
    local_exp = local_part.at[export_flat].add(returned.reshape(devices * slot_count, coeffs))
    far_part = jnp.sum(local_exp.T[:, :, None] * monomial, axis=0)
    stacked = jnp.concatenate([positions, masses[None, :]], axis=0)
    extended = padded(stacked, ((("group", "dom"), 1),), RIM * LEAF_SIZE)
    own_leaves = stacked.reshape(4, leaves, LEAF_SIZE).transpose(1, 0, 2)
    ext_leaves = extended.reshape(4, leaves + 2 * RIM, LEAF_SIZE).transpose(1, 0, 2)
    near_part = near_field(own_leaves, ext_leaves, near_target, near_source, near_count[0])
    return (near_part + far_part).reshape(-1)


def solution(mesh):
    in_specs = (
        P(None, ("group", "dom")),
        P(("group", "dom")),
        P(("group", "dom")),
        P(("group", "dom")),
        P(("group", "dom")),
        P(("group", "dom")),
        P(("group", "dom")),
        P(("group", "dom")),
        P(("group", "dom")),
        P(("group", "dom"), None),
        P(),
    )
    out_specs = P(("group", "dom"))
    return jax.shard_map(local, mesh=mesh, in_specs=in_specs, out_specs=out_specs, check_vma=False)
```

profile of v0, /device:TPU:1, one launch (start us, length us, event | category | flops | bytes accessed | tf_op | source)
XLA Modules:
  0.0 676.5 jit_solution(17139056105994012286)
XLA Ops:
  1.3 4.5 collective-permute-start
  67.1 6.0 multiply_reduce_fusion.3
  73.2 5.5 gather_fusion.2
  79.9 8.8 %all-to-all-start = ((f32[8,32,672]{2,1,0:T(8,128)}), f32[8,32,672]{2,1,0:T(8,128)}, u32[]{:S(2)}, u32[]{:S(2)}) async-start(f32[8,32,672]{2,1,0:T(8,128)} %reshape.187), calls=%async_computation | async-start | bytes 1572864 | tf_op jit(solution)/shard_map/all_to_all | solution.py:158
  89.7 8.7 %gather_fusion.4 = f32[128,7056]{1,0:T(8,128)} fusion(f32[316,7056]{1,0:T(8,128)} %param.24, s32[1024]{0:T(1024)S(1)} %pad_clamp_fusion.2), kind=kCustom, calls=%fused_computation.4 | custom fusion | bytes 7225856 | tf_op jit(solution)/shard_map/gather | solution.py:79
  98.4 6.3 reshape.283
  104.7 54.5 %gather_fusion.5 = f32[16384,84]{1,0:T(8,128)} fusion(f32[512,84]{1,0:T(8,128)S(1)} %bitcast.39, s32[16384]{0:T(1024)S(1)} %get-tuple-element.132), kind=kCustom, calls=%fused_computation.5 | custom fusion | bytes 11075584 | tf_op jit(solution)/shard_map/gather | solution.py:84
  159.1 8.7 %copy.153 = f32[128,128,84]{1,2,0:T(8,128)} copy(f32[128,128,84]{2,1,0:T(8,128)} %bitcast.43) | data formatting | bytes 11010048 | tf_op jit(solution)/shard_map/reshape | solution.py:84
  167.9 14.1 %multiply_multiply_fusion = f32[128,128,84]{1,2,0:T(8,128)} fusion(f32[128,84,84]{2,1,0:T(8,128)} %reshape.283, f32[128,128,84]{1,2,0:T(8,128)} %copy.153, f32[84]{0:T(128)S(1)} %copy-done.6, f32[128,128]{1,0:T(8,128)S(1)} %fusion.17), kind=kOutput, calls=%fused_computation.20 | convolution fusion | flops 1391394816 | bytes 14688592 | tf_op jit(solution)/shard_map/nkj,nbj->nbk/dot_general | solution.py:91
  184.5 8.3 %copy.166 = f32[128,128,84]{2,1,0:T(8,128)} copy(f32[128,128,84]{1,2,0:T(8,128)} %multiply_multiply_fusion) | data formatting | bytes 11010048 | tf_op jit(solution)/shard_map/reshape | solution.py:104
  192.8 88.0 %scatter_custom_fusion.2 = f32[2048,84]{1,0:T(8,128)S(1)} fusion(s32[16384]{0:T(1024)S(1)} %get-tuple-element.134, f32[16384,84]{1,0:T(8,128)} %bitcast.47, f32[]{:T(128)} %constant.7.clone.1), kind=kCustom, calls=%fused_computation.27 | custom fusion | flops 1376256 | bytes 688640 | tf_op jit(solution)/shard_map/scatter-add | solution.py:104
  282.1 6.6 all-to-all-start.2
  290.4 2.5 copy.144
  292.9 12.1 %all-to-all-done.2 = f32[8,32,672]{2,1,0:T(8,128)} async-done(((f32[8,32,672]{2,1,0:T(8,128)}), f32[8,32,672]{2,1,0:T(8,128)}, u32[]{:S(2)}, u32[]{:S(2)}) %all-to-all-start.2) | async-done | bytes 688160 | tf_op jit(solution)/shard_map/all_to_all | solution.py:170
  305.0 14.8 %all-to-all-start.1 = ((f32[8,32,672]{2,0,1:T(8,128)}), f32[8,32,672]{2,0,1:T(8,128)}, u32[]{:S(2)}, u32[]{:S(2)}) async-start(f32[8,32,672]{2,0,1:T(8,128)} %copy.144), calls=%async_computation.1 | async-start | bytes 1572864 | tf_op jit(solution)/shard_map/all_to_all | solution.py:157
  319.8 152.8 %while.10 = (s32[]{:T(128)}, f32[512,64]{1,0:T(8,128)S(1)}, s32[16,256]{1,0:T(8,128)}, f32[512,4,64]{2,1,0:T(4,128)S(1)}, s32[16,256]{1,0:T(8,128)}, /*index=5*/...) while((s32[]{:T(128)}, f32[512,64]{1,0:T(8,128)S(1)}, s32[16,256]{1,0:T(8,128)}, ...), condition=%wide.region_4.0_spmd, body=%wide.region_0.4_spmd.sunk | while | flops 13668354 | bytes 11489393 | solution.py:132
  327.3 2.0 scatter_fusion
  336.9 2.0 scatter_fusion
  346.4 2.0 scatter_fusion
  356.0 2.0 scatter_fusion
  365.5 2.0 scatter_fusion
  375.1 2.0 scatter_fusion
  422.8 2.0 scatter_fusion
  441.9 2.0 scatter_fusion
  472.7 2.5 copy.157
  475.2 7.7 %all-to-all-start.3 = ((f32[8,32,672]{2,0,1:T(8,128)}), f32[8,32,672]{2,0,1:T(8,128)S(1)}, u32[]{:S(2)}, u32[]{:S(2)}) async-start(f32[8,32,672]{2,0,1:T(8,128)} %copy.157), calls=%async_computation.3 | async-start | bytes 1572864 | tf_op jit(solution)/shard_map/all_to_all | solution.py:169
  484.8 54.5 %gather_fusion.3 = f32[16384,84]{1,0:T(8,128)} fusion(f32[2048,84]{1,0:T(8,128)S(1)} %reshape.188, s32[16384]{0:T(1024)S(1)} %get-tuple-element.135), kind=kCustom, calls=%fused_computation.3 | custom fusion | bytes 11075584 | tf_op jit(solution)/shard_map/gather | solution.py:83
  539.3 21.4 %broadcast_multiply_fusion = f32[128,128,84]{1,2,0:T(8,128)} fusion(f32[128,128]{1,0:T(8,128)S(1)} %fusion.17, f32[128,128,84]{2,1,0:T(8,128)} %bitcast.44, f32[128,84,84]{2,1,0:T(8,128)} %reshape.283), kind=kOutput, calls=%fused_computation.24 | convolution fusion | flops 1388642304 | bytes 14688256 | tf_op jit(solution)/shard_map/nkj,nbj->nbk/dot_general | solution.py:87
  560.7 8.3 %copy.163 = f32[128,128,84]{2,1,0:T(8,128)} copy(f32[128,128,84]{1,2,0:T(8,128)} %broadcast_multiply_fusion) | data formatting | bytes 11010048 | tf_op jit(solution)/shard_map/reshape | solution.py:99
  569.7 87.7 %scatter_custom_fusion.1 = f32[512,84]{1,0:T(8,128)S(1)} fusion(s32[16384]{0:T(1024)} %get-tuple-element.133, f32[16384,84]{1,0:T(8,128)} %bitcast.46, f32[]{:T(128)} %constant.7.clone.1), kind=kCustom, calls=%fused_computation.114 | custom fusion | flops 1376256 | bytes 172544 | tf_op jit(solution)/shard_map/scatter-add | solution.py:99
  657.4 11.8 %scatter_fusion.1 = f32[512,84]{1,0:T(8,128)S(1)} fusion(f32[512,84]{1,0:T(8,128)S(1)} %scatter_custom_fusion.1, s32[2048]{0:T(1024)S(1)} %bitcast.56, f32[2048,84]{1,0:T(8,128)S(1)} %reshape.274), kind=kCustom, calls=%fused_computation.9 | custom fusion | flops 172032 | bytes 2072576 | tf_op jit(solution)/shard_map/scatter-add | solution.py:176
  669.4 5.9 multiply_reduce_fusion.2
  (376 shorter events, 208.8 us)
Async XLA Ops:
  1.3 287.5 %collective-permute-start = (f32[4,128]{1,0:T(4,128)}, f32[4,128]{1,0:T(4,128)S(1)}, u32[]{:S(2)}, u32[]{:S(2)}) collective-permute-start(f32[4,128]{1,0:T(4,128)} %get-tuple-element.130), channel_id=1, source_target_pairs={{0,1},{1,2},{2,3},{3,4},{4,5},{5,6},{6,7},{7,8},{8,9},{9,10},{10,1... | collective-permute-start | bytes 6152 | tf_op jit(solution)/shard_map/ppermute | solution.py:25
  5.8 283.0 %collective-permute-start.1 = (f32[4,128]{1,0:T(4,128)S(1)}, f32[4,128]{1,0:T(4,128)}, u32[]{:S(2)}, u32[]{:S(2)}) collective-permute-start(f32[4,128]{1,0:T(4,128)S(1)} %get-tuple-element.131), channel_id=1, source_target_pairs={{1,0},{2,1},{3,2},{4,3},{5,4},{6,5},{7,6},{8,7},{9,8},{10,9},{11,1... | collective-permute-start | bytes 6152 | tf_op jit(solution)/shard_map/ppermute | solution.py:27
  66.4 22.3 %copy-start.1 = (f32[32768]{0:T(1024)S(1)}, f32[32768]{0:T(1024)}, u32[]{:S(2)}) copy-start(f32[32768]{0:T(1024)} %param.15) | copy-start | bytes 393220
  67.1 21.7 %copy-start.8 = (s32[128]{0:T(128)S(1)}, s32[128]{0:T(128)}, u32[]{:S(2)}) copy-start(s32[128]{0:T(128)} %param.21) | copy-start | bytes 1540
  67.1 21.8 %copy-start.7 = (s32[128]{0:T(128)S(1)}, s32[128]{0:T(128)}, u32[]{:S(2)}) copy-start(s32[128]{0:T(128)} %param.22) | copy-start | bytes 1540
  67.1 21.9 %copy-start.2 = (s32[16384]{0:T(1024)S(1)}, s32[16384]{0:T(1024)}, u32[]{:S(2)}) copy-start(s32[16384]{0:T(1024)} %param.19) | copy-start | bytes 196612
  79.9 202.2 %all-to-all-start = ((f32[8,32,672]{2,1,0:T(8,128)}), f32[8,32,672]{2,1,0:T(8,128)}, u32[]{:S(2)}, u32[]{:S(2)}) async-start(f32[8,32,672]{2,1,0:T(8,128)} %reshape.187), calls=%async_computation | async-start | bytes 1572864 | tf_op jit(solution)/shard_map/all_to_all | solution.py:158
  159.1 8.7 %copy-start.3 = (s32[16384]{0:T(1024)S(1)}, s32[16384]{0:T(1024)}, u32[]{:S(2)}) copy-start(s32[16384]{0:T(1024)} %param.20) | copy-start | bytes 196612
  159.1 8.7 %copy-start.6 = (f32[84]{0:T(128)S(1)}, f32[84]{0:T(128)}, u32[]{:S(2)}) copy-start(f32[84]{0:T(128)} %constant.31.clone) | copy-start | bytes 1012
  167.8 14.8 %copy-start.4 = (s32[4096]{0:T(1024)S(1)}, s32[4096]{0:T(1024)}, u32[]{:S(2)}) copy-start(s32[4096]{0:T(1024)} %param.16) | copy-start | bytes 49156
  167.8 15.4 %copy-start.5 = (s32[4096]{0:T(1024)S(1)}, s32[4096]{0:T(1024)}, u32[]{:S(2)}) copy-start(s32[4096]{0:T(1024)} %param.17) | copy-start | bytes 49156
  182.0 106.8 %copy-start = (f32[3,32768]{1,0:T(4,128)S(1)}, f32[3,32768]{1,0:T(4,128)}, u32[]{:S(2)}) copy-start(f32[3,32768]{1,0:T(4,128)} %param.14) | copy-start | bytes 1179652
  282.1 22.9 %all-to-all-start.2 = ((f32[8,32,672]{2,1,0:T(8,128)}), f32[8,32,672]{2,1,0:T(8,128)}, u32[]{:S(2)}, u32[]{:S(2)}) async-start(f32[8,32,672]{2,1,0:T(8,128)} %reshape.194), calls=%async_computation.2 | async-start | bytes 1572864 | tf_op jit(solution)/shard_map/all_to_all | solution.py:170
  305.0 170.2 %all-to-all-start.1 = ((f32[8,32,672]{2,0,1:T(8,128)}), f32[8,32,672]{2,0,1:T(8,128)}, u32[]{:S(2)}, u32[]{:S(2)}) async-start(f32[8,32,672]{2,0,1:T(8,128)} %copy.144), calls=%async_computation.1 | async-start | bytes 1572864 | tf_op jit(solution)/shard_map/all_to_all | solution.py:157
  475.2 93.8 %all-to-all-start.3 = ((f32[8,32,672]{2,0,1:T(8,128)}), f32[8,32,672]{2,0,1:T(8,128)S(1)}, u32[]{:S(2)}, u32[]{:S(2)}) async-start(f32[8,32,672]{2,0,1:T(8,128)} %copy.157), calls=%async_computation.3 | async-start | bytes 1572864 | tf_op jit(solution)/shard_map/all_to_all | solution.py:169
where the time goes:
time: 685 us; the launch traced here: 676 us
  other arithmetic  367 us (54%)
  local copies, waits for them, and re-layouts  215 us (31%)
  starting transfers between devices  44.3 us (6%)
  matrix products  35.5 us (5%)
  waiting for transfers between devices  12.1 us (2%)
    scatter-add x1, other arithmetic, far_terms(): reaction = jnp.zeros((received.shape[0], coeffs), jnp.float32).at[far_sou...  88 us
    scatter-add x1, other arithmetic, far_terms(): local_part = jnp.zeros((multipole.shape[1], coeffs), jnp.float32).at[far_...  87.7 us
    gather x1, local copies, waits for them, and re-layouts, far_terms(): source_rows = received[far_source].reshape(batches, batch_size, coeffs)  54.5 us
    gather x1, local copies, waits for them, and re-layouts, far_terms(): target_rows = multipole.T[far_target].reshape(batches, batch_size, coeffs)  54.5 us
    unnamed x80, other arithmetic  53.9 us
    scatter-add x16, other arithmetic, one_block(): return (totals.at[target_ids].add(potential_part), None)  32.8 us
    reduce_sum x16, other arithmetic, one_block(): distance = jnp.sum(offsets * offsets, axis=1)  27.6 us
    convert_element_type x16, other arithmetic, one_block(): (position_ids < live_count).astype(jnp.float32)[:, None]  21.7 us
  transfers between devices with their start and end apart: 6, of which 1 were waited for; matrix products, arithmetic and copies ran while one was open for 75% of the time, Pallas kernels for 0%

commit v1 on v0

v1 whole, which is shorter than its diff:
```python
import functools

import jax
import jax.numpy as jnp
import numpy as np
from jax import lax
from jax.experimental import pallas as pl
from jax.experimental.pallas import tpu as pltpu
from jax.sharding import PartitionSpec as P

LEAF = 64
ORDER = 6
LANES = 128
SOFTENING = 0.01
ACCS = 4
GROUP = 8
MIB = 1 << 20


def exponent_table(degree_max):
    triples = []
    for degree in range(degree_max + 1):
        for first_pow in range(degree, -1, -1):
            for second_pow in range(degree - first_pow, -1, -1):
                triples.append((first_pow, second_pow, degree - first_pow - second_pow))
    return triples


TRIPLES = exponent_table(ORDER)
COEFFS = len(TRIPLES)
INDEX = {triple: k for k, triple in enumerate(TRIPLES)}
SIGNS = np.ones((1, LANES), np.float32)
SIGNS[0, :COEFFS] = [(-1.0) ** sum(triple) for triple in TRIPLES]


def split(value):
    high = value.astype(jnp.bfloat16)
    return high, (value - high.astype(jnp.float32)).astype(jnp.bfloat16)


def dot_t(a, b):
    return lax.dot_general(a, b, (((1,), (1,)), ((), ())), preferred_element_type=jnp.float32)


def lane_id(shape):
    return lax.broadcasted_iota(jnp.int32, shape, len(shape) - 1)


def walk(x, y, z, start, visit):
    along_x = start
    for a in range(ORDER + 1):
        along_y = along_x
        for b in range(ORDER + 1 - a):
            along_z = along_y
            for c in range(ORDER + 1 - a - b):
                visit(INDEX[(a, b, c)], along_z)
                if c < ORDER - a - b:
                    along_z = along_z * z
            if b < ORDER - a:
                along_y = along_y * y
        if a < ORDER:
            along_x = along_x * x


def multipole_kernel(slots, pos, mass, table, exports, turned, terms):
    rows = mass.shape[0]
    for c in range(3):
        turned[c] = pos[c].T
    turned[3] = mass[...].T
    terms[...] = jnp.zeros_like(terms)
    for half in range(2):
        for block in range(rows // LANES):
            here = (slice(half * LEAF, (half + 1) * LEAF), slice(block * LANES, (block + 1) * LANES))
            u = []
            for c in range(3):
                value = turned[(c,) + here]
                u.append(value - jnp.sum(value, axis=0, keepdims=True) * (1.0 / LEAF))

            def visit(k, value, half=half, here=here):
                terms[half, k : k + 1, here[1]] = jnp.sum(value, axis=0, keepdims=True)

            walk(*u, turned[(3,) + here], visit)
    for half in range(2):
        table[pl.ds(half, rows, 2), :] = terms[half].T

    def export(group, carry):
        for i in range(GROUP):
            place = group * GROUP + i
            exports[pl.ds(place, 1), :] = table[pl.ds(slots[place], 1), :]
        return carry

    lax.fori_loop(0, exports.shape[0] // GROUP, export, 0)


def operator_kernel(classes, operators, out, rows, sem):
    batches = rows.shape[0]

    def copy(n):
        return pltpu.make_async_copy(operators.at[pl.ds(classes[n], 1), :], rows.at[pl.ds(n, 1), :], sem)

    lax.fori_loop(0, batches, lambda n, c: (copy(n).start(), c)[1], 0)
    lax.fori_loop(0, batches, lambda n, c: (copy(n).wait(), c)[1], 0)
    lane = lane_id((GROUP, LANES))

    def spread(group, carry):
        here = pl.ds(pl.multiple_of(group * GROUP, GROUP), GROUP)
        for k in range(COEFFS):
            first, offset = divmod(k * COEFFS, LANES)
            width = rows.shape[1]
            value = rows[here, first * LANES : min((first + 1) * LANES, width)]
            if value.shape[1] < LANES:
                value = jnp.concatenate([value, jnp.zeros((GROUP, LANES - value.shape[1]), jnp.float32)], axis=1)
            if offset:
                value = pltpu.roll(value, LANES - offset, 1)
            if offset + COEFFS > LANES:
                later = rows[here, (first + 1) * LANES : min((first + 2) * LANES, width)]
                if later.shape[1] < LANES:
                    later = jnp.concatenate(
                        [later, jnp.zeros((GROUP, LANES - later.shape[1]), jnp.float32)], axis=1
                    )
                value = jnp.where(lane < LANES - offset, value, pltpu.roll(later, LANES - offset, 1))
            out[here, k, :] = jnp.where(lane < COEFFS, value, 0.0)
        return carry

    lax.fori_loop(0, batches // GROUP, spread, 0)
    out[:, COEFFS:, :] = jnp.zeros((batches, LANES - COEFFS, LANES), jnp.float32)


def far_kernel(signed, counts, sources, targets, signs, table, matrix, out, held, *totals):
    batches = matrix.shape[0]
    size = held.shape[0] // batches

    def gather(n, carry):
        def step(group, carry):
            first = n * size + group * GROUP
            for i in range(GROUP):
                held[pl.ds(first + i, 1), :] = table[pl.ds(sources[first + i], 1), :]
            return carry

        return lax.fori_loop(0, (counts[n] + GROUP - 1) // GROUP, step, carry)

    lax.fori_loop(0, batches, gather, 0)
    row = lax.broadcasted_iota(jnp.int32, (size, LANES), 0)

    def product(n, carry):
        here = pl.ds(pl.multiple_of(n * size, size), size)
        value = jnp.where(row < counts[n], held[here, :], 0.0)
        if signed:
            value = value * signs[...]
        high, low = split(value)
        matrix_high, matrix_low = split(matrix[n])
        result = dot_t(high, matrix_high) + dot_t(low, matrix_high) + dot_t(high, matrix_low)
        held[here, :] = result * signs[...] if signed else result
        return carry

    lax.fori_loop(0, batches, product, 0, unroll=4)
    for total in totals:
        total[...] = jnp.zeros_like(total)

    def scatter(n, carry):
        def step(group, carry):
            first = n * size + group * GROUP
            for i in range(GROUP):
                total = totals[i % len(totals)]
                there = pl.ds(targets[first + i], 1)
                total[there, :] = total[there, :] + held[pl.ds(first + i, 1), :]
            return carry

        return lax.fori_loop(0, (counts[n] + GROUP - 1) // GROUP, step, carry)

    lax.fori_loop(0, batches, scatter, 0)
    out[...] = functools.reduce(lambda a, b: a + b, [total[...] for total in totals])


def near_kernel(targets, sources, count, pos, mass, before, after, out, extended, mixed, ahead, source, target, total):
    rows = mass.shape[0]
    lane = lane_id((GROUP, LANES))
    wide = lane_id((rows, LANES))
    for c in range(4):
        own = pos[c] if c < 3 else mass[...]
        extended[c, rows : extended.shape[1], :] = jnp.zeros((extended.shape[1] - rows, LANES), jnp.float32)
        extended[c, 1 : rows + 1, :] = own
        extended[c, 0:1, :] = before[c : c + 1, :]
        extended[c, rows + 1 : rows + 2, :] = after[c : c + 1, :]
        if c < 3:
            swapped = pltpu.roll(own, LEAF, 1)
            ahead[c, pl.ds(0, rows, 2), :] = jnp.where(wide < LEAF, own, swapped)
            ahead[c, pl.ds(1, rows, 2), :] = jnp.where(wide < LEAF, swapped, own)
    for c in range(4):
        for block in range(mixed.shape[0]):
            turned = extended[c, (block // 2) * LANES : (block // 2 + 1) * LANES, :].T
            for parity in range(2):
                for q in range(4):
                    first = parity * LEAF + q * GROUP
                    low = turned[first : first + GROUP]
                    high = turned[first + LEAF // 2 : first + LEAF // 2 + GROUP]
                    if block % 2:
                        low = pltpu.roll(low, LEAF, 1)
                    else:
                        high = pltpu.roll(high, LEAF, 1)
                    mixed[block, parity, c * 4 + q] = jnp.where(lane < LEAF, low, high)
    base = jnp.where(lane < LEAF, 0, LEAF)

    def spread(r, carry):
        pick = base + r % LEAF
        for parity in range(2):
            for part in range(16):
                source[2 * r + parity, part] = jnp.take_along_axis(mixed[r // LEAF, parity, part], pick, axis=1)
        return carry

    lax.fori_loop(0, rows + 2, spread, 0)

    def spread_target(leaf, carry):
        for c in range(3):
            target[leaf, c] = jnp.broadcast_to(ahead[c, pl.ds(leaf, 1), :], (GROUP, LANES))
        return carry

    lax.fori_loop(0, 2 * rows, spread_target, 0, unroll=4)
    total[...] = jnp.zeros_like(total)

    def pair(j):
        here, there = targets[j], sources[j]
        x, y, z = target[here, 0], target[here, 1], target[here, 2]
        parts = []
        for q in range(4):
            dx = x - source[there, q]
            dy = y - source[there, 4 + q]
            dz = z - source[there, 8 + q]
            distance = dx * dx + dy * dy + dz * dz
            inverse = jnp.where(distance > 0.0, lax.rsqrt(distance + SOFTENING), 0.0)
            parts.append(inverse * source[there, 12 + q])
        return here, (parts[0] + parts[1]) + (parts[2] + parts[3])

    def several(group, carry):
        done = [pair(group * GROUP + i) for i in range(GROUP)]
        for here, value in done:
            total[here] = total[here] + value
        return carry

    def single(j, carry):
        here, value = pair(j)
        total[here] = total[here] + value
        return carry

    live = count[0]
    full = live // GROUP
    lax.fori_loop(0, full, several, 0)
    lax.fori_loop(full * GROUP, live, single, 0)
    summed = jnp.sum(total[...], axis=1)
    ahead[0] = summed + pltpu.roll(summed, LEAF, 1)
    out[...] = -jnp.where(wide < LEAF, ahead[0, pl.ds(0, rows, 2), :], ahead[0, pl.ds(1, rows, 2), :])


def evaluate_kernel(pos, local, returned, slots, near, out, expansion, turned, terms):
    rows = near.shape[0]
    leaves = local.shape[0]
    chunk = slots.shape[1]
    leaf = lax.broadcasted_iota(jnp.int32, (leaves, chunk), 0)
    sums = local[...]
    for block in range(slots.shape[0]):
        hot = (leaf == slots[block : block + 1, :]).astype(jnp.float32).astype(jnp.bfloat16)
        high, low = split(returned[block * chunk : (block + 1) * chunk, :])
        sums = sums + jnp.dot(hot, high, preferred_element_type=jnp.float32)
        sums = sums + jnp.dot(hot, low, preferred_element_type=jnp.float32)
    expansion[...] = sums
    for half in range(2):
        terms[half] = expansion[pl.ds(half, rows, 2), :].T
    for c in range(3):
        turned[c] = pos[c].T
    for half in range(2):
        for block in range(rows // LANES):
            here = (slice(half * LEAF, (half + 1) * LEAF), slice(block * LANES, (block + 1) * LANES))
            u = []
            for c in range(3):
                value = turned[(c,) + here]
                u.append(value - jnp.sum(value, axis=0, keepdims=True) * (1.0 / LEAF))
            sums = [jnp.zeros((LEAF, LANES), jnp.float32)]

            def visit(k, value, half=half, here=here, sums=sums):
                sums[0] = sums[0] + value * terms[half, k : k + 1, here[1]]

            walk(*u, jnp.ones((LEAF, LANES), jnp.float32), visit)
            turned[(3,) + here] = sums[0]
    out[...] = near[...] + turned[3].T


VMEM = pl.BlockSpec(memory_space=pltpu.VMEM)
SMEM = pl.BlockSpec(memory_space=pltpu.SMEM)
ANY = pl.BlockSpec(memory_space=pl.ANY)


def shape(*dims):
    return jax.ShapeDtypeStruct(dims, jnp.float32)


def params(mib):
    return pltpu.CompilerParams(vmem_limit_bytes=mib * MIB)


def multipoles(pos, mass, slots):
    rows = mass.shape[0]
    return pl.pallas_call(
        multipole_kernel,
        out_shape=(shape(2 * rows, LANES), shape(slots.shape[0], LANES)),
        in_specs=[SMEM, VMEM, VMEM],
        out_specs=(VMEM, VMEM),
        scratch_shapes=[pltpu.VMEM((4, LANES, rows), jnp.float32), pltpu.VMEM((2, LANES, rows), jnp.float32)],
        compiler_params=params(32),
        name="multipoles",
    )(slots, pos, mass)


def operator_matrices(classes, operators):
    batches = classes.shape[0]
    return pl.pallas_call(
        operator_kernel,
        out_shape=shape(batches, LANES, LANES),
        in_specs=[SMEM, ANY],
        out_specs=VMEM,
        scratch_shapes=[pltpu.VMEM((batches, operators.shape[1]), jnp.float32), pltpu.SemaphoreType.DMA],
        compiler_params=params(32),
        name="operator_matrices",
    )(classes, operators)


def far(signed, counts, sources, targets, table, matrix, out_rows, name):
    return pl.pallas_call(
        functools.partial(far_kernel, signed),
        out_shape=shape(out_rows, LANES),
        in_specs=[SMEM, SMEM, SMEM, VMEM, VMEM, VMEM],
        out_specs=VMEM,
        scratch_shapes=[pltpu.VMEM((sources.shape[0], LANES), jnp.float32)]
        + [pltpu.VMEM((out_rows, LANES), jnp.float32)] * ACCS,
        compiler_params=params(48),
        name=name,
    )(counts, sources, targets, jnp.asarray(SIGNS), table, matrix)


def near_field(targets, sources, count, pos, mass, before, after):
    rows = mass.shape[0]
    blocks = -(-(rows + 2) // LEAF)
    return pl.pallas_call(
        near_kernel,
        out_shape=shape(rows, LANES),
        in_specs=[SMEM, SMEM, SMEM, VMEM, VMEM, VMEM, VMEM],
        out_specs=VMEM,
        scratch_shapes=[
            pltpu.VMEM((4, (blocks + 1) // 2 * LANES, LANES), jnp.float32),
            pltpu.VMEM((blocks, 2, 16, GROUP, LANES), jnp.float32),
            pltpu.VMEM((3, 2 * rows, LANES), jnp.float32),
            pltpu.VMEM((2 * rows + 4, 16, GROUP, LANES), jnp.float32),
            pltpu.VMEM((2 * rows, 3, GROUP, LANES), jnp.float32),
            pltpu.VMEM((2 * rows, GROUP, LANES), jnp.float32),
        ],
        compiler_params=params(58),
        name="near_field",
    )(targets, sources, count, pos, mass, before, after)


def evaluate(pos, local, returned, slots, near):
    rows = near.shape[0]
    return pl.pallas_call(
        evaluate_kernel,
        out_shape=shape(rows, LANES),
        in_specs=[VMEM] * 5,
        out_specs=VMEM,
        scratch_shapes=[
            pltpu.VMEM((2 * rows, LANES), jnp.float32),
            pltpu.VMEM((4, LANES, rows), jnp.float32),
            pltpu.VMEM((2, LANES, rows), jnp.float32),
        ],
        compiler_params=params(32),
        name="evaluate",
    )(pos, local, returned, slots, near)


AXES = ("group", "dom")


def exchange(value):
    return lax.all_to_all(value, AXES, split_axis=0, concat_axis=0, tiled=True)


def shift(value, forward):
    count = lax.axis_size("group") * lax.axis_size("dom")
    pairs = [(i, i + 1) for i in range(count - 1)] if forward else [(i + 1, i) for i in range(count - 1)]
    return lax.ppermute(value, AXES, pairs)


def local(
    positions,
    masses,
    near_target,
    near_source,
    near_count,
    far_target,
    far_source,
    far_class,
    far_count,
    export_slots,
    operators,
):
    devices = lax.axis_size("group") * lax.axis_size("dom")
    slots = export_slots.reshape(-1)
    pos = positions.reshape(3, -1, LANES)
    mass = masses.reshape(-1, LANES)
    leaves = masses.shape[0] // LEAF
    ends = jnp.concatenate([pos[:, :: mass.shape[0] - 1], mass[None, :: mass.shape[0] - 1]], axis=0)
    before = shift(ends[:, 1], True)
    after = shift(ends[:, 0], False)
    table, exports = multipoles(pos, mass, slots)
    received = exchange(exports.reshape(devices, -1, LANES)).reshape(-1, LANES)
    matrix = operator_matrices(far_class, operators)
    reaction = far(True, far_count, far_target, far_source, table, matrix, slots.shape[0], "far_reaction")
    returned = exchange(reaction.reshape(devices, -1, LANES)).reshape(-1, LANES)
    near = near_field(near_target, near_source, near_count, pos, mass, before, after)
    local_part = far(False, far_count, far_source, far_target, received, matrix, leaves, "far_local")
    out = evaluate(pos, local_part, returned, slots.reshape(8, -1), near)
    return out.reshape(-1)


def solution(mesh):
    split_all = P(AXES)
    in_specs = (P(None, AXES),) + (split_all,) * 8 + (P(AXES, None), P())
    return jax.shard_map(local, mesh=mesh, in_specs=in_specs, out_specs=split_all, check_vma=False)
```

time: 685 us -> 248 us (0.36)
  the two profiles are of different devices: /device:TPU:1 before, /device:TPU:224 now
where the time goes in v1:
time: 248 us
  Pallas kernels  182 us (73%)
  starting transfers between devices  38.1 us (15%)
  waiting for transfers between devices  14.4 us (6%)
  local copies, waits for them, and re-layouts  12.6 us (5%)
    pallas_call x2, Pallas kernels, far(): pl.pallas_call(functools.partial(far_kernel, signed), out_shape=shape(out...  96.7 us
    pallas_call x1, Pallas kernels, near_field(): pl.pallas_call(near_kernel, out_shape=shape(rows, LANES), in_specs=[SMEM,...  66.1 us
    all_to_all x2, starting transfers between devices, exchange(): return lax.all_to_all(value, AXES, split_axis=0, concat_axis=0, tiled=True)  28.2 us
    ppermute x2, waiting for transfers between devices, shift(): return lax.ppermute(value, AXES, pairs)  14.4 us
    unnamed x28, local copies, waits for them, and re-layouts  11.4 us
    pallas_call x1, Pallas kernels, operator_matrices(): pl.pallas_call(operator_kernel, out_shape=shape(batches, LANES, LANES), i...  10.2 us
    ppermute x2, starting transfers between devices, shift(): return lax.ppermute(value, AXES, pairs)  9.91 us
    pallas_call x1, Pallas kernels, multipoles(): pl.pallas_call(multipole_kernel, out_shape=(shape(2 * rows, LANES), shape...  5.81 us
  transfers between devices with their start and end apart: 4, of which 1 were waited for; matrix products, arithmetic and copies ran while one was open for 0% of the time, Pallas kernels for 70%

profile of v1, /device:TPU:224, one launch (start us, length us, event | category | flops | bytes accessed | tf_op | source)
XLA Modules:
  0.0 247.8 jit_solution(4561163042534321652)
XLA Ops:
  0.0 1.1 copy.18
  1.1 0.0 copy-start.2
  1.1 0.8 copy.14
  1.9 0.1 reshape.25.slots
  2.0 0.0 copy-start.4
  2.1 0.9 copy-done.4
  3.0 5.8 %multipoles.1 = (f32[512,128]{1,0:T(8,128)S(1)}, f32[2048,128]{1,0:T(8,128)}) custom-call(s32[2048]{0:T(1024)S(1)} %reshape.25.slots, f32[3,256,128]{2,1,0:T(8,128)S(1)} %bitcast.13, f32[256,128]{1,0:T(8,128)S(1)} %bitcast.21), custom_call_target="tpu_custom_call" | custom-call | tf_op jit(solution)/shard_map/multipoles/pallas_call | solution.py:302
  8.8 13.3 %all-to-all-start = ((f32[256,8,128]{2,1,0:T(8,128)}), f32[256,8,128]{2,1,0:T(8,128)S(1)}, u32[]{:S(2)}, u32[]{:S(2)}) async-start(f32[256,8,128]{2,1,0:T(8,128)} %bitcast.1), calls=%async_computation | async-start | bytes 2097152 | tf_op jit(solution)/shard_map/all_to_all | solution.py:381
  22.0 0.0 copy-start.1
  22.1 3.6 %copy-done.1 = f32[316,7056]{1,0:T(8,128)S(1)} copy-done((f32[316,7056]{1,0:T(8,128)S(1)}, f32[316,7056]{1,0:T(8,128)}, u32[]{:S(2)}) %copy-start.1) | copy-done | bytes 8918808
  25.7 0.7 copy-done.10
  26.3 10.2 %operator_matrices.1.matrix = f32[128,128,128]{2,1,0:T(8,128)S(1)} custom-call(s32[128]{0:T(128)S(1)} %copy-done.10, f32[316,7056]{1,0:T(8,128)S(1)} %copy-done.1), custom_call_target="tpu_custom_call" | custom-call | tf_op jit(solution)/shard_map/operator_matrices/pallas_call | solution.py:315
  36.5 0.0 copy-start
  36.5 3.2 %copy-done = f32[128,128,128]{2,1,0:T(8,128)} copy-done((f32[128,128,128]{2,1,0:T(8,128)}, f32[128,128,128]{2,1,0:T(8,128)S(1)}, u32[]{:S(2)}) %copy-start) | copy-done | bytes 8388632
  39.7 0.0 copy-done.6
  39.7 0.0 copy-done.9
  39.7 49.1 %far_reaction.1 = f32[2048,128]{1,0:T(8,128)} custom-call(s32[128]{0:T(128)S(1)} %copy-done.8, s32[16384]{0:T(1024)S(1)} %copy-done.7, s32[16384]{0:T(1024)S(1)} %copy-done.6, f32[1,128]{1,0:T(1,128)S(1)} %copy-done.9, f32[512,128]{1,0:T(8,128)S(1)} %get-tuple-element.8.table, f32[128,128,128]{2,1,0:T(8,128)} %copy-done), custom_call_target="tpu_custom_call" | custom-call | tf_op jit(solution)/shard_map/far_reaction/pallas_call | solution.py:327
  88.8 0.0 all-to-all-done
  88.8 14.9 %all-to-all-start.1 = ((f32[256,8,128]{2,1,0:T(8,128)}), f32[256,8,128]{2,1,0:T(8,128)S(1)}, u32[]{:S(2)}, u32[]{:S(2)}) async-start(f32[256,8,128]{2,1,0:T(8,128)} %bitcast.3), calls=%async_computation.1 | async-start | bytes 2097152 | tf_op jit(solution)/shard_map/all_to_all | solution.py:381
  103.8 0.9 slice.13
  104.7 0.0 copy-done.2
  104.7 2.2 collective-permute-start
  106.9 7.7 %collective-permute-start.1 = (f32[4,128]{1,0:T(4,128)S(1)}, f32[4,128]{1,0:T(4,128)S(1)}, u32[]{:S(2)}, u32[]{:S(2)}) collective-permute-start(f32[4,128]{1,0:T(4,128)S(1)} %bitcast.24), channel_id=1, source_target_pairs={{1,0},{2,1},{3,2},{4,3},{5,4},{6,5},{7,6},{8,7},{9,8},{10,9},{11,1... | collective-permute-start | bytes 6152 | tf_op jit(solution)/shard_map/ppermute | solution.py:387
  114.7 0.1 reshape_reshape.3.slots
  115.4 14.4 %collective-permute-done.before = f32[4,128]{1,0:T(4,128)S(1)} collective-permute-done((f32[4,128]{1,0:T(4,128)S(1)}, f32[4,128]{1,0:T(4,128)S(1)}, u32[]{:S(2)}, u32[]{:S(2)}) %collective-permute-start) | collective-permute-done | bytes 2080 | tf_op jit(solution)/shard_map/ppermute | solution.py:387
  129.8 0.0 collective-permute-done.1.after
  129.8 0.6 copy-done.11
  130.4 0.5 copy-done.12
  130.9 66.1 %near_field.1.near = f32[256,128]{1,0:T(8,128)} custom-call(s32[4096]{0:T(1024)} %targets.5, s32[4096]{0:T(1024)} %sources.5, s32[1]{0:T(128)S(6)} %copy.19.count, f32[3,256,128]{2,1,0:T(8,128)} %bitcast.15, f32[256,128]{1,0:T(8,128)} %bitcast.20, f32[4,128]{1,0:T(4,128)} %copy-done.11, f32[4,128]{1,0:T(4,128)} %copy-done.12), custom_call_target="tpu_custom_call" | custom-call | tf_op jit(solution)/shard_map/near_field/pallas_call | solution.py:342
  197.0 47.6 %far_local.1.local = f32[512,128]{1,0:T(8,128)S(1)} custom-call(s32[128]{0:T(128)S(1)} %copy-done.8, s32[16384]{0:T(1024)S(1)} %copy-done.6, s32[16384]{0:T(1024)S(1)} %copy-done.7, f32[1,128]{1,0:T(1,128)S(1)} %copy-done.9, f32[2048,128]{1,0:T(8,128)S(1)} %bitcast.17, f32[128,128,128]{2,1,0:T(8,128)} %copy-done), custom_call_target="tpu_custom_call" | custom-call | tf_op jit(solution)/shard_map/far_local/pallas_call | solution.py:327
  244.6 0.0 all-to-all-done.1
  244.7 3.2 %evaluate.1 = f32[256,128]{1,0:T(8,128)} custom-call(f32[3,256,128]{2,1,0:T(8,128)S(1)} %bitcast.16, f32[512,128]{1,0:T(8,128)S(1)} %far_local.1.local, f32[2048,128]{1,0:T(8,128)S(1)} %bitcast.18, s32[8,256]{1,0:T(8,128)S(1)} %reshape_reshape.3.slots, f32[256,128]{1,0:T(8,128)S(1)} %copy-done.5), custom_call_target="tpu_custom_call" | custom-call | tf_op jit(solution)/shard_map/evaluate/pallas_call | solution.py:362
  (15 shorter events, 0.1 us)
Async XLA Ops:
  1.1 103.6 %copy-start.2 = (f32[1,3,256,128]{3,2,1,0:T(8,128)}, f32[1,3,256,128]{3,2,1,0:T(8,128)S(1)}, u32[]{:S(2)}) copy-start(f32[1,3,256,128]{3,2,1,0:T(8,128)S(1)} %copy.18) | copy-start | bytes 1179652
  2.0 0.9 copy-start.4
  8.8 80.1 %all-to-all-start = ((f32[256,8,128]{2,1,0:T(8,128)}), f32[256,8,128]{2,1,0:T(8,128)S(1)}, u32[]{:S(2)}, u32[]{:S(2)}) async-start(f32[256,8,128]{2,1,0:T(8,128)} %bitcast.1), calls=%async_computation | async-start | bytes 2097152 | tf_op jit(solution)/shard_map/all_to_all | solution.py:381
  22.0 3.6 %copy-start.1 = (f32[316,7056]{1,0:T(8,128)S(1)}, f32[316,7056]{1,0:T(8,128)}, u32[]{:S(2)}) copy-start(f32[316,7056]{1,0:T(8,128)} %operators.1) | copy-start | bytes 26756356
  25.7 0.7 copy-start.10
  26.3 13.4 %copy-start.6 = (s32[16384]{0:T(1024)S(1)}, s32[16384]{0:T(1024)}, u32[]{:S(2)}) copy-start(s32[16384]{0:T(1024)} %targets.4) | copy-start | bytes 196612
  26.3 13.4 %copy-start.7 = (s32[16384]{0:T(1024)S(1)}, s32[16384]{0:T(1024)}, u32[]{:S(2)}) copy-start(s32[16384]{0:T(1024)} %sources.4) | copy-start | bytes 196612
  26.3 13.4 %copy-start.8 = (s32[128]{0:T(128)S(1)}, s32[128]{0:T(128)}, u32[]{:S(2)}) copy-start(s32[128]{0:T(128)} %counts.3) | copy-start | bytes 1540
  26.3 13.4 %copy-start.9 = (f32[1,128]{1,0:T(1,128)S(1)}, f32[1,128]{1,0:T(1,128)}, u32[]{:S(2)}) copy-start(f32[1,128]{1,0:T(1,128)} %constant.2.clone.signs) | copy-start | bytes 1540
  36.5 3.2 %copy-start = (f32[128,128,128]{2,1,0:T(8,128)}, f32[128,128,128]{2,1,0:T(8,128)S(1)}, u32[]{:S(2)}) copy-start(f32[128,128,128]{2,1,0:T(8,128)S(1)} %operator_matrices.1.matrix) | copy-start | bytes 25165828
  88.8 155.8 %all-to-all-start.1 = ((f32[256,8,128]{2,1,0:T(8,128)}), f32[256,8,128]{2,1,0:T(8,128)S(1)}, u32[]{:S(2)}, u32[]{:S(2)}) async-start(f32[256,8,128]{2,1,0:T(8,128)} %bitcast.3), calls=%async_computation.1 | async-start | bytes 2097152 | tf_op jit(solution)/shard_map/all_to_all | solution.py:381
  104.7 139.9 %copy-start.3 = (f32[1,3,256,128]{3,2,1,0:T(8,128)S(1)}, f32[1,3,256,128]{3,2,1,0:T(8,128)}, u32[]{:S(2)}) copy-start(f32[1,3,256,128]{3,2,1,0:T(8,128)} %copy-done.2) | copy-start | bytes 1179652
  104.7 25.1 %collective-permute-start = (f32[4,128]{1,0:T(4,128)S(1)}, f32[4,128]{1,0:T(4,128)S(1)}, u32[]{:S(2)}, u32[]{:S(2)}) collective-permute-start(f32[4,128]{1,0:T(4,128)S(1)} %bitcast.25), channel_id=1, source_target_pairs={{0,1},{1,2},{2,3},{3,4},{4,5},{5,6},{6,7},{7,8},{8,9},{9,10},{10,1... | collective-permute-start | bytes 6152 | tf_op jit(solution)/shard_map/ppermute | solution.py:387
  106.9 22.9 %collective-permute-start.1 = (f32[4,128]{1,0:T(4,128)S(1)}, f32[4,128]{1,0:T(4,128)S(1)}, u32[]{:S(2)}, u32[]{:S(2)}) collective-permute-start(f32[4,128]{1,0:T(4,128)S(1)} %bitcast.24), channel_id=1, source_target_pairs={{1,0},{2,1},{3,2},{4,3},{5,4},{6,5},{7,6},{8,7},{9,8},{10,9},{11,1... | collective-permute-start | bytes 6152 | tf_op jit(solution)/shard_map/ppermute | solution.py:387
  129.8 0.6 copy-start.11
  130.4 0.5 copy-start.12
  197.0 47.6 %copy-start.5 = (f32[256,128]{1,0:T(8,128)S(1)}, f32[256,128]{1,0:T(8,128)}, u32[]{:S(2)}) copy-start(f32[256,128]{1,0:T(8,128)} %near_field.1.near) | copy-start | bytes 393220

commit v2 on v1

v2 whole, which is shorter than its diff:
```python
import functools

import jax
import jax.numpy as jnp
import numpy as np
from jax import lax
from jax.experimental import pallas as pl
from jax.experimental.pallas import tpu as pltpu
from jax.sharding import PartitionSpec as P

LEAF = 64
ORDER = 6
LANES = 128
SOFTENING = 0.01
ACCS = 8
GROUP = 8
ROWS = 16
PAIRS = 16
JOINT = 4
MIB = 1 << 20


def exponent_table(degree_max):
    triples = []
    for degree in range(degree_max + 1):
        for first_pow in range(degree, -1, -1):
            for second_pow in range(degree - first_pow, -1, -1):
                triples.append((first_pow, second_pow, degree - first_pow - second_pow))
    return triples


TRIPLES = exponent_table(ORDER)
COEFFS = len(TRIPLES)
INDEX = {triple: k for k, triple in enumerate(TRIPLES)}
SIGNS = np.ones((1, LANES), np.float32)
SIGNS[0, :COEFFS] = [(-1.0) ** sum(triple) for triple in TRIPLES]


def split(value):
    high = value.astype(jnp.bfloat16)
    return high, (value - high.astype(jnp.float32)).astype(jnp.bfloat16)


def dot_t(a, b):
    return lax.dot_general(a, b, (((1,), (1,)), ((), ())), preferred_element_type=jnp.float32)


def lane_id(shape):
    return lax.broadcasted_iota(jnp.int32, shape, len(shape) - 1)


def walk(x, y, z, start, visit):
    along_x = start
    for a in range(ORDER + 1):
        along_y = along_x
        for b in range(ORDER + 1 - a):
            along_z = along_y
            for c in range(ORDER + 1 - a - b):
                visit(INDEX[(a, b, c)], along_z)
                if c < ORDER - a - b:
                    along_z = along_z * z
            if b < ORDER - a:
                along_y = along_y * y
        if a < ORDER:
            along_x = along_x * x


def centred(turned, here):
    u = []
    for c in range(3):
        value = turned[(c,) + here]
        u.append(value - jnp.sum(value, axis=0, keepdims=True) * (1.0 / LEAF))
    return u


def blocks_of(rows):
    for half in range(2):
        for block in range(rows // LANES):
            yield half, (slice(half * LEAF, (half + 1) * LEAF), slice(block * LANES, (block + 1) * LANES))


def list_groups(counts, batches, size, groups):
    def one(n, place):
        for i in range(size // ROWS):
            groups[place + i] = n * size + i * ROWS
        return place + (counts[n] + ROWS - 1) // ROWS

    return lax.fori_loop(0, batches, one, 0)


def each_group(groups, number, step):
    def several(turn, carry):
        step([groups[turn * JOINT + i] for i in range(JOINT)])
        return carry

    def single(turn, carry):
        step([groups[turn]])
        return carry

    lax.fori_loop(0, number // JOINT, several, 0)
    lax.fori_loop(number // JOINT * JOINT, number, single, 0)


def views(index):
    return [index.at[pl.ds(i, index.shape[0] - ROWS + 1)] for i in range(ROWS)]


def gather_rows(groups, number, index, table, held):
    later = views(index)

    def step(firsts):
        for first in firsts:
            rows = [table[pl.ds(later[i][first], 1), :] for i in range(ROWS)]
            for i in range(ROWS):
                held[pl.ds(first + i, 1), :] = rows[i]

    each_group(groups, number, step)


def scatter_rows(groups, number, index, held, totals):
    for total in totals:
        total[...] = jnp.zeros_like(total)

    later = views(index)

    def step(firsts):
        for first in firsts:
            for i in range(ROWS):
                total = totals[i % len(totals)]
                there = pl.ds(later[i][first], 1)
                total[there, :] = total[there, :] + held[pl.ds(first + i, 1), :]

    each_group(groups, number, step)


def sum_of(totals):
    return functools.reduce(lambda a, b: a + b, [total[...] for total in totals])


def multiply(value, both):
    high, low = split(value)
    wide = dot_t(high, both)
    return wide[:, :LANES] + wide[:, LANES:] + dot_t(low, both[:LANES])


def front_kernel(
    slots, classes, counts, targets, sources, signs, pos, mass, operators,
    message, packed,
    turned, terms, table, rows, matrix, both, held, *rest,
):
    *totals, groups, row_sem, out_sem = rest
    batches = rows.shape[0]
    size = held.shape[0] // batches
    leaf_rows = mass.shape[0]

    def fetch(n):
        return pltpu.make_async_copy(operators.at[pl.ds(classes[n], 1), :], rows.at[pl.ds(n, 1), :], row_sem)

    lax.fori_loop(0, batches, lambda n, c: (fetch(n).start(), c)[1], 0)
    for c in range(3):
        turned[c] = pos[c].T
    turned[3] = mass[...].T
    terms[...] = jnp.zeros_like(terms)
    for half, here in blocks_of(leaf_rows):

        def visit(k, value, half=half, here=here):
            terms[half, k : k + 1, here[1]] = jnp.sum(value, axis=0, keepdims=True)

        walk(*centred(turned, here), turned[(3,) + here], visit)
    for half in range(2):
        table[pl.ds(half, leaf_rows, 2), :] = terms[half].T
    cap = message.shape[1] // 2

    later = views(slots)

    def export(group, carry):
        values = [table[pl.ds(later[i][group * ROWS], 1), :] for i in range(ROWS)]
        for i in range(ROWS):
            message[group * (ROWS // cap) + i // cap, i % cap : i % cap + 1, :] = values[i]
        return carry

    lax.fori_loop(0, slots.shape[0] // ROWS, export, 0)
    number = list_groups(counts, batches, size, groups)
    gather_rows(groups, number, targets, table, held)
    lax.fori_loop(0, batches, lambda n, c: (fetch(n).wait(), c)[1], 0)
    lane = lane_id((GROUP, LANES))
    width = rows.shape[1]
    matrix[:, COEFFS:, :] = jnp.zeros((batches, LANES - COEFFS, LANES), jnp.float32)

    def spread(group, carry):
        here = pl.ds(pl.multiple_of(group * GROUP, GROUP), GROUP)

        def part(first):
            value = rows[here, first * LANES : min((first + 1) * LANES, width)]
            if value.shape[1] < LANES:
                value = jnp.concatenate([value, jnp.zeros((GROUP, LANES - value.shape[1]), jnp.float32)], axis=1)
            return value

        for k in range(COEFFS):
            first, offset = divmod(k * COEFFS, LANES)
            value = part(first)
            if offset + COEFFS > LANES:
                value = jnp.where(lane < offset, part(first + 1), value)
            if offset:
                value = pltpu.roll(value, LANES - offset, 1)
            matrix[here, k, :] = jnp.where(lane < COEFFS, value, 0.0)
        return carry

    lax.fori_loop(0, batches // GROUP, spread, 0)
    row = lax.broadcasted_iota(jnp.int32, (size, LANES), 0)

    def product(n, carry):
        here = pl.ds(pl.multiple_of(n * size, size), size)
        value = jnp.where(row < counts[n], held[here, :], 0.0) * signs[...]
        high, low = split(matrix[n])
        both[n, :LANES] = high
        both[n, LANES:] = low
        held[here, :] = multiply(value, jnp.concatenate([high, low], axis=0))
        return carry

    lax.fori_loop(0, batches, product, 0, unroll=8)
    save = pltpu.make_async_copy(both, packed, out_sem)
    save.start()
    scatter_rows(groups, number, sources, held, totals)
    message[:, cap:, :] = (sum_of(totals) * signs[...]).reshape(message.shape[0], cap, LANES)
    save.wait()


def near_kernel(targets, sources, count, pos, mass, before, after, out, extended, lines, choose, ahead, source, target, total):
    rows = mass.shape[0]
    wide = lane_id((rows, LANES))
    for c in range(4):
        own = pos[c] if c < 3 else mass[...]
        extended[c, rows : extended.shape[1], :] = jnp.zeros((extended.shape[1] - rows, LANES), jnp.float32)
        extended[c, 1 : rows + 1, :] = own
        extended[c, 0:1, :] = before[c : c + 1, :]
        extended[c, rows + 1 : rows + 2, :] = after[c : c + 1, :]
        if c < 3:
            swapped = pltpu.roll(own, LEAF, 1)
            ahead[c, pl.ds(0, rows, 2), :] = jnp.where(wide < LEAF, own, swapped)
            ahead[c, pl.ds(1, rows, 2), :] = jnp.where(wide < LEAF, swapped, own)
    k_id = lax.broadcasted_iota(jnp.int32, (2 * LANES, 2 * LANES), 0)
    n_id = lax.broadcasted_iota(jnp.int32, (2 * LANES, 2 * LANES), 1)
    k_in = k_id % LANES
    code = (k_in // (3 * GROUP)) * GROUP + k_in % GROUP - n_id // LANES * GROUP
    code = jnp.where(k_id // LANES == n_id % LANES // LEAF, code, -1)
    tiles = choose.shape[0]

    def make_choice(tile, carry):
        wanted = tile // GROUP * 2 * GROUP + tile % GROUP
        choose[tile] = (code == wanted).astype(jnp.float32).astype(jnp.bfloat16)
        return carry

    lax.fori_loop(0, tiles, make_choice, 0)
    blocks = lines.shape[0] // LEAF
    for block in range(blocks):
        parts = []
        for c in range(4):
            value = extended[c, block * GROUP : (block + 1) * GROUP, :]
            for _ in range(2):
                high = value.astype(jnp.bfloat16).astype(jnp.float32)
                parts.append(high)
                value = value - high
            parts.append(value)
        parts.append(jnp.zeros((LANES - 12 * GROUP, LANES), jnp.float32))
        turned = jnp.concatenate(parts, axis=0).T.astype(jnp.bfloat16)
        quarter = LEAF // 2
        for parity in range(2):
            there = slice(block * LEAF + parity * quarter, block * LEAF + (parity + 1) * quarter)
            lines[there, :LANES] = turned[parity * LEAF : parity * LEAF + quarter]
            lines[there, LANES:] = turned[parity * LEAF + quarter : (parity + 1) * LEAF]
    share = blocks // 3

    def spread(step, carry):
        tile, third = step % tiles, step // tiles
        pair_of, r = tile // GROUP, tile % GROUP
        size = share * LEAF
        some = lines[pl.ds(pl.multiple_of(third * size, size), size), :]
        wide = jnp.dot(some, choose[tile], preferred_element_type=jnp.float32)
        for i in range(share):
            for parity in range(2):
                for q in range(4):
                    first = i * LEAF + parity * 32 + q * GROUP
                    leaf = 2 * ((third * share + i) * GROUP + r) + parity
                    for c in range(2):
                        source[leaf, (2 * pair_of + c) * 4 + q] = wide[first : first + GROUP, c * LANES : (c + 1) * LANES]
        return carry

    lax.fori_loop(0, 3 * tiles, spread, 0, unroll=2)

    def spread_target(leaf, carry):
        for c in range(3):
            target[leaf, c] = jnp.broadcast_to(ahead[c, pl.ds(leaf, 1), :], (GROUP, LANES))
        return carry

    lax.fori_loop(0, 2 * rows, spread_target, 0, unroll=4)
    total[...] = jnp.zeros_like(total)

    def pair(here, there):
        x, y, z = target[here, 0], target[here, 1], target[here, 2]
        parts = []
        for q in range(4):
            dx = x - source[there, q]
            dy = y - source[there, 4 + q]
            dz = z - source[there, 8 + q]
            distance = dx * dx + dy * dy + dz * dz
            inverse = jnp.where(distance > 0.0, lax.rsqrt(distance + SOFTENING), 0.0)
            parts.append(inverse * source[there, 12 + q])
        return here, (parts[0] + parts[1]) + (parts[2] + parts[3])

    later_target, later_source = views(targets), views(sources)

    def several(group, carry):
        first = group * PAIRS
        done = [pair(later_target[i][first], later_source[i][first]) for i in range(PAIRS)]
        for here, value in done:
            total[here] = total[here] + value
        return carry

    def single(j, carry):
        here, value = pair(targets[j], sources[j])
        total[here] = total[here] + value
        return carry

    live = count[0]
    full = live // PAIRS
    lax.fori_loop(0, full, several, 0)
    lax.fori_loop(full * PAIRS, live, single, 0)
    summed = jnp.sum(total[...], axis=1)
    ahead[0] = summed + pltpu.roll(summed, LEAF, 1)
    out[...] = -jnp.where(wide < LEAF, ahead[0, pl.ds(0, rows, 2), :], ahead[0, pl.ds(1, rows, 2), :])


def back_kernel(
    counts, sources, targets, slots, pos, near, packed, message,
    out,
    table, returned, both, held, expansion, turned, terms, *rest,
):
    *totals, groups, matrix_sem, table_sem, returned_sem = rest
    cap = table.shape[1]
    batches = both.shape[0]
    size = held.shape[0] // batches
    rows = near.shape[0]
    fetch_table = pltpu.make_async_copy(message.at[:, :cap, :], table, table_sem)
    fetch_table.start()
    fetch_returned = pltpu.make_async_copy(message.at[:, cap:, :], returned, returned_sem)
    fetch_returned.start()
    fetch_matrix = pltpu.make_async_copy(packed, both, matrix_sem)
    fetch_matrix.start()
    for c in range(3):
        turned[c] = pos[c].T
    number = list_groups(counts, batches, size, groups)
    fetch_table.wait()
    gather_rows(groups, number, sources, table.reshape(table.shape[0] * cap, LANES), held)
    fetch_matrix.wait()
    row = lax.broadcasted_iota(jnp.int32, (size, LANES), 0)

    def product(n, carry):
        here = pl.ds(pl.multiple_of(n * size, size), size)
        held[here, :] = multiply(jnp.where(row < counts[n], held[here, :], 0.0), both[n])
        return carry

    lax.fori_loop(0, batches, product, 0, unroll=8)
    scatter_rows(groups, number, targets, held, totals)
    fetch_returned.wait()
    chunk = slots.shape[1]
    leaf = lax.broadcasted_iota(jnp.int32, (expansion.shape[0], chunk), 0)
    sums = sum_of(totals)
    for block in range(slots.shape[0]):
        hot = (leaf == slots[block : block + 1, :]).astype(jnp.float32).astype(jnp.bfloat16)
        part = returned[block * chunk // cap : (block + 1) * chunk // cap]
        high, low = split(part.reshape(chunk, LANES))
        sums = sums + jnp.dot(hot, high, preferred_element_type=jnp.float32)
        sums = sums + jnp.dot(hot, low, preferred_element_type=jnp.float32)
    expansion[...] = sums
    for half in range(2):
        terms[half] = expansion[pl.ds(half, rows, 2), :].T
    for half, here in blocks_of(rows):
        sums = [jnp.zeros((LEAF, LANES), jnp.float32)]

        def visit(k, value, half=half, here=here, sums=sums):
            sums[0] = sums[0] + value * terms[half, k : k + 1, here[1]]

        walk(*centred(turned, here), jnp.ones((LEAF, LANES), jnp.float32), visit)
        turned[(3,) + here] = sums[0]
    out[...] = near[...] + turned[3].T


VMEM = pl.BlockSpec(memory_space=pltpu.VMEM)
SMEM = pl.BlockSpec(memory_space=pltpu.SMEM)
ANY = pl.BlockSpec(memory_space=pl.ANY)


def shape(*dims):
    return jax.ShapeDtypeStruct(dims, jnp.float32)


def params(mib):
    return pltpu.CompilerParams(vmem_limit_bytes=mib * MIB)


def scratch(*dims, dtype=jnp.float32):
    return pltpu.VMEM(dims, dtype)


def group_list(pairs, batches):
    return pltpu.SMEM((pairs // ROWS + pairs // batches // ROWS,), jnp.int32)


def front(slots, classes, counts, targets, sources, pos, mass, operators, devices):
    rows = mass.shape[0]
    batches, pairs = classes.shape[0], targets.shape[0]
    return pl.pallas_call(
        front_kernel,
        out_shape=(
            shape(devices, 2 * slots.shape[0] // devices, LANES),
            jax.ShapeDtypeStruct((batches, 2 * LANES, LANES), jnp.bfloat16),
        ),
        in_specs=[SMEM] * 5 + [VMEM] * 3 + [ANY],
        out_specs=(VMEM, ANY),
        scratch_shapes=[
            scratch(4, LANES, rows),
            scratch(2, LANES, rows),
            scratch(2 * rows, LANES),
            scratch(batches, operators.shape[1]),
            scratch(batches, LANES, LANES),
            scratch(batches, 2 * LANES, LANES, dtype=jnp.bfloat16),
            scratch(pairs, LANES),
        ]
        + [scratch(slots.shape[0], LANES)] * ACCS
        + [group_list(pairs, batches)]
        + [pltpu.SemaphoreType.DMA] * 2,
        compiler_params=params(58),
        name="front",
    )(slots, classes, counts, targets, sources, jnp.asarray(SIGNS), pos, mass, operators)


def back(counts, sources, targets, slots, pos, near, packed, message):
    rows = near.shape[0]
    cap = message.shape[1] // 2
    return pl.pallas_call(
        back_kernel,
        out_shape=shape(rows, LANES),
        in_specs=[SMEM] * 3 + [VMEM] * 3 + [ANY] * 2,
        out_specs=VMEM,
        scratch_shapes=[
            scratch(message.shape[0], cap, LANES),
            scratch(message.shape[0], cap, LANES),
            scratch(*packed.shape, dtype=jnp.bfloat16),
            scratch(sources.shape[0], LANES),
            scratch(2 * rows, LANES),
            scratch(4, LANES, rows),
            scratch(2, LANES, rows),
        ]
        + [scratch(2 * rows, LANES)] * ACCS
        + [group_list(sources.shape[0], counts.shape[0])]
        + [pltpu.SemaphoreType.DMA] * 3,
        compiler_params=params(58),
        name="back",
    )(counts, sources, targets, slots, pos, near, packed, message)


def near_field(targets, sources, count, pos, mass, before, after):
    rows = mass.shape[0]
    blocks = -(-(rows + 2) // (3 * GROUP)) * 3
    return pl.pallas_call(
        near_kernel,
        out_shape=shape(rows, LANES),
        in_specs=[SMEM] * 3 + [VMEM] * 4,
        out_specs=VMEM,
        scratch_shapes=[
            scratch(4, blocks * GROUP, LANES),
            scratch(blocks * LEAF, 2 * LANES, dtype=jnp.bfloat16),
            scratch(2 * GROUP, 2 * LANES, 2 * LANES, dtype=jnp.bfloat16),
            scratch(3, 2 * rows, LANES),
            scratch(2 * blocks * GROUP, 16, GROUP, LANES),
            scratch(2 * rows, 3, GROUP, LANES),
            scratch(2 * rows, GROUP, LANES),
        ],
        compiler_params=params(58),
        name="near_field",
    )(targets, sources, count, pos, mass, before, after)


AXES = ("group", "dom")


def exchange(value):
    return lax.all_to_all(value, AXES, split_axis=0, concat_axis=0, tiled=True)


def shift(value, forward):
    count = lax.axis_size("group") * lax.axis_size("dom")
    pairs = [(i, i + 1) for i in range(count - 1)] if forward else [(i + 1, i) for i in range(count - 1)]
    return lax.ppermute(value, AXES, pairs)


def local(
    positions,
    masses,
    near_target,
    near_source,
    near_count,
    far_target,
    far_source,
    far_class,
    far_count,
    export_slots,
    operators,
):
    devices = lax.axis_size("group") * lax.axis_size("dom")
    slots = export_slots.reshape(-1)
    pos = positions.reshape(3, -1, LANES)
    mass = masses.reshape(-1, LANES)
    ends = jnp.concatenate([pos[:, :: mass.shape[0] - 1], mass[None, :: mass.shape[0] - 1]], axis=0)
    before = shift(ends[:, 1], True)
    after = shift(ends[:, 0], False)
    message, packed = front(slots, far_class, far_count, far_target, far_source, pos, mass, operators, devices)
    message = exchange(message)
    near = near_field(near_target, near_source, near_count, pos, mass, before, after)
    out = back(far_count, far_source, far_target, slots.reshape(8, -1), pos, near, packed, message)
    return out.reshape(-1)


def solution(mesh):
    split_all = P(AXES)
    in_specs = (P(None, AXES),) + (split_all,) * 8 + (P(AXES, None), P())
    return jax.shard_map(local, mesh=mesh, in_specs=in_specs, out_specs=split_all, check_vma=False)
```

time: 248 us -> 187 us (0.75)
  the two profiles are of different devices: /device:TPU:224 before, /device:TPU:160 now
where the time goes in v2:
time: 187 us
  Pallas kernels  118 us (63%)
  waiting for transfers between devices  36.3 us (19%)
  starting transfers between devices  23.3 us (12%)
  local copies, waits for them, and re-layouts  8.48 us (5%)
    pallas_call x1, Pallas kernels, near_field(): pl.pallas_call(near_kernel, out_shape=shape(rows, LANES), in_specs=[SMEM]...  47.9 us
    pallas_call x1, Pallas kernels, front(): pl.pallas_call(front_kernel, out_shape=(shape(devices, 2 * slots.shape[0]...  39 us
    ppermute x2, waiting for transfers between devices, shift(): return lax.ppermute(value, AXES, pairs)  36.3 us
    pallas_call x1, Pallas kernels, back(): pl.pallas_call(back_kernel, out_shape=shape(rows, LANES), in_specs=[SMEM]...  31 us
    all_to_all x1, starting transfers between devices, exchange(): return lax.all_to_all(value, AXES, split_axis=0, concat_axis=0, tiled=True)  13.5 us
    ppermute x2, starting transfers between devices, shift(): return lax.ppermute(value, AXES, pairs)  9.78 us
    unnamed x8, local copies, waits for them, and re-layouts  5.13 us
  transfers between devices with their start and end apart: 3, of which 1 were waited for; matrix products, arithmetic and copies ran while one was open for 1% of the time, Pallas kernels for 26%

profile of v2, /device:TPU:160, one launch (start us, length us, event | category | flops | bytes accessed | tf_op | source)
XLA Modules:
  0.0 186.8 jit_solution(1605712448387568342)
XLA Ops:
  0.0 0.8 copy.14
  0.8 0.7 reshape.14.slots
  1.5 1.9 copy.18
  3.4 39.0 %front.1 = (f32[256,16,128]{2,1,0:T(8,128)}, bf16[128,256,128]{2,1,0:T(8,128)(2,1)}) custom-call(s32[2048]{0:T(1024)} %reshape.14.slots, s32[128]{0:T(128)} %classes.1, s32[128]{0:T(128)} %counts.3, s32[16384]{0:T(1024)} %targets.5, s32[16384]{0:T(1024)} %sources.5, f32[1,128]{1,0:T(1,128)} %constant.2.clone.signs, f32[3,256,128]{2,1,0:T(8,128)} %bitcast.9, ...), custom_call_target="tpu_custom_call" | custom-call | tf_op jit(solution)/shard_map/front/pallas_call | solution.py:413
  42.4 13.5 %all-to-all-start = ((f32[256,16,128]{2,1,0:T(8,128)}), f32[256,16,128]{2,1,0:T(8,128)S(1)}, u32[]{:S(2)}, u32[]{:S(2)}) async-start(f32[256,16,128]{2,1,0:T(8,128)} %get-tuple-element.8), calls=%async_computation | async-start | bytes 4194304 | tf_op jit(solution)/shard_map/all_to_all | solution.py:489
  55.9 0.9 slice.13
  56.8 1.0 slice.12
  57.8 2.1 %collective-permute-start = (f32[4,128]{1,0:T(4,128)S(1)}, f32[4,128]{1,0:T(4,128)S(1)}, u32[]{:S(2)}, u32[]{:S(2)}) collective-permute-start(f32[4,128]{1,0:T(4,128)S(1)} %bitcast.19), channel_id=1, source_target_pairs={{0,1},{1,2},{2,3},{3,4},{4,5},{5,6},{6,7},{7,8},{8,9},{9,10},{10,1... | collective-permute-start | bytes 6152 | tf_op jit(solution)/shard_map/ppermute | solution.py:495
  59.9 7.7 %collective-permute-start.1 = (f32[4,128]{1,0:T(4,128)S(1)}, f32[4,128]{1,0:T(4,128)S(1)}, u32[]{:S(2)}, u32[]{:S(2)}) collective-permute-start(f32[4,128]{1,0:T(4,128)S(1)} %bitcast.18), channel_id=1, source_target_pairs={{1,0},{2,1},{3,2},{4,3},{5,4},{6,5},{7,6},{8,7},{9,8},{10,9},{11,1... | collective-permute-start | bytes 6152 | tf_op jit(solution)/shard_map/ppermute | solution.py:495
  67.6 0.7 reshape_reshape.3.slots
  69.0 36.3 %collective-permute-done.before = f32[4,128]{1,0:T(4,128)S(1)} collective-permute-done((f32[4,128]{1,0:T(4,128)S(1)}, f32[4,128]{1,0:T(4,128)S(1)}, u32[]{:S(2)}, u32[]{:S(2)}) %collective-permute-start) | collective-permute-done | bytes 2080 | tf_op jit(solution)/shard_map/ppermute | solution.py:495
  105.3 0.0 copy-start.1
  105.3 0.0 collective-permute-done.1.after
  105.3 0.6 copy-done.1
  105.9 0.0 copy-start.2
  105.9 0.5 copy-done.2
  106.4 47.9 %near_field.1.near = f32[256,128]{1,0:T(8,128)} custom-call(s32[4096]{0:T(1024)} %targets.3, s32[4096]{0:T(1024)} %sources.3, s32[1]{0:T(128)S(6)} %copy.19.count, f32[3,256,128]{2,1,0:T(8,128)} %bitcast.11, f32[256,128]{1,0:T(8,128)} %bitcast.15, f32[4,128]{1,0:T(4,128)} %copy-done.1, f32[4,128]{1,0:T(4,128)} %copy-done.2), custom_call_target="tpu_custom_call" | custom-call | tf_op jit(solution)/shard_map/near_field/pallas_call | solution.py:466
  154.4 0.0 all-to-all-done.message
  154.4 0.0 copy-start
  154.4 1.4 copy-done
  155.7 31.0 %back.1 = f32[256,128]{1,0:T(8,128)} custom-call(s32[128]{0:T(128)} %counts.3, s32[16384]{0:T(1024)} %sources.5, s32[16384]{0:T(1024)} %targets.5, s32[8,256]{1,0:T(8,128)} %reshape_reshape.3.slots, f32[3,256,128]{2,1,0:T(8,128)} %bitcast.12, f32[256,128]{1,0:T(8,128)} %near_field.1.near, bf16[128,256,128]{2,1,0:T(8,128)(2,1)} %get-tuple-element.7.packed, ...), custom_call_target="tpu_custom_call" | custom-call | tf_op jit(solution)/shard_map/back/pallas_call | solution.py:441
  (1 shorter events, 0.0 us)
Async XLA Ops:
  42.4 112.0 %all-to-all-start = ((f32[256,16,128]{2,1,0:T(8,128)}), f32[256,16,128]{2,1,0:T(8,128)S(1)}, u32[]{:S(2)}, u32[]{:S(2)}) async-start(f32[256,16,128]{2,1,0:T(8,128)} %get-tuple-element.8), calls=%async_computation | async-start | bytes 4194304 | tf_op jit(solution)/shard_map/all_to_all | solution.py:489
  57.8 47.5 %collective-permute-start = (f32[4,128]{1,0:T(4,128)S(1)}, f32[4,128]{1,0:T(4,128)S(1)}, u32[]{:S(2)}, u32[]{:S(2)}) collective-permute-start(f32[4,128]{1,0:T(4,128)S(1)} %bitcast.19), channel_id=1, source_target_pairs={{0,1},{1,2},{2,3},{3,4},{4,5},{5,6},{6,7},{7,8},{8,9},{9,10},{10,1... | collective-permute-start | bytes 6152 | tf_op jit(solution)/shard_map/ppermute | solution.py:495
  59.9 45.4 %collective-permute-start.1 = (f32[4,128]{1,0:T(4,128)S(1)}, f32[4,128]{1,0:T(4,128)S(1)}, u32[]{:S(2)}, u32[]{:S(2)}) collective-permute-start(f32[4,128]{1,0:T(4,128)S(1)} %bitcast.18), channel_id=1, source_target_pairs={{1,0},{2,1},{3,2},{4,3},{5,4},{6,5},{7,6},{8,7},{9,8},{10,9},{11,1... | collective-permute-start | bytes 6152 | tf_op jit(solution)/shard_map/ppermute | solution.py:495
  105.3 0.6 copy-start.1
  105.9 0.5 copy-start.2
  154.4 1.4 copy-start

commit v3 on v2

--- a/solution.py
+++ b/solution.py
@@ -15,7 +15,7 @@
 ACCS = 8
 GROUP = 8
 ROWS = 16
-PAIRS = 16
+PAIRS = 32
 JOINT = 4
 MIB = 1 << 20
 
@@ -39,10 +39,6 @@
 def split(value):
     high = value.astype(jnp.bfloat16)
     return high, (value - high.astype(jnp.float32)).astype(jnp.bfloat16)
-
-
-def dot_t(a, b):
-    return lax.dot_general(a, b, (((1,), (1,)), ((), ())), preferred_element_type=jnp.float32)
 
 
 def lane_id(shape):
@@ -101,12 +97,12 @@
     lax.fori_loop(number // JOINT * JOINT, number, single, 0)
 
 
-def views(index):
-    return [index.at[pl.ds(i, index.shape[0] - ROWS + 1)] for i in range(ROWS)]
+def views(index, width):
+    return [index.at[pl.ds(i, index.shape[0] - width + 1)] for i in range(width)]
 
 
 def gather_rows(groups, number, index, table, held):
-    later = views(index)
+    later = views(index, ROWS)
 
     def step(firsts):
         for first in firsts:
@@ -121,7 +117,7 @@
     for total in totals:
         total[...] = jnp.zeros_like(total)
 
-    later = views(index)
+    later = views(index, ROWS)
 
     def step(firsts):
         for first in firsts:
@@ -137,10 +133,13 @@
     return functools.reduce(lambda a, b: a + b, [total[...] for total in totals])
 
 
+def dot(a, b):
+    return jnp.dot(a, b, preferred_element_type=jnp.float32)
+
+
 def multiply(value, both):
     high, low = split(value)
-    wide = dot_t(high, both)
-    return wide[:, :LANES] + wide[:, LANES:] + dot_t(low, both[:LANES])
+    return dot(high, both[:LANES]) + dot(low, both[:LANES]) + dot(high, both[LANES:])
 
 
 def front_kernel(
@@ -171,7 +170,7 @@
         table[pl.ds(half, leaf_rows, 2), :] = terms[half].T
     cap = message.shape[1] // 2
 
-    later = views(slots)
+    later = views(slots, ROWS)
 
     def export(group, carry):
         values = [table[pl.ds(later[i][group * ROWS], 1), :] for i in range(ROWS)]
@@ -212,7 +211,7 @@
     def product(n, carry):
         here = pl.ds(pl.multiple_of(n * size, size), size)
         value = jnp.where(row < counts[n], held[here, :], 0.0) * signs[...]
-        high, low = split(matrix[n])
+        high, low = split(matrix[n].T)
         both[n, :LANES] = high
         both[n, LANES:] = low
         held[here, :] = multiply(value, jnp.concatenate([high, low], axis=0))
@@ -308,7 +307,7 @@
             parts.append(inverse * source[there, 12 + q])
         return here, (parts[0] + parts[1]) + (parts[2] + parts[3])
 
-    later_target, later_source = views(targets), views(sources)
+    later_target, later_source = views(targets, PAIRS), views(sources, PAIRS)
 
     def several(group, carry):
         first = group * PAIRS
@@ -516,6 +515,7 @@
     before = shift(ends[:, 1], True)
     after = shift(ends[:, 0], False)
     message, packed = front(slots, far_class, far_count, far_target, far_source, pos, mass, operators, devices)
+    message, before, after = lax.optimization_barrier((message, before, after))
     message = exchange(message)
     near = near_field(near_target, near_source, near_count, pos, mass, before, after)
     out = back(far_count, far_source, far_target, slots.reshape(8, -1), pos, near, packed, message)

time: 187 us -> 148 us (0.79)
  the two profiles are of different devices: /device:TPU:160 before, /device:TPU:1 now
where the time goes in v3:
time: 148 us; the launch traced here: 147 us
  Pallas kernels  109 us (74%)
  starting transfers between devices  22.3 us (15%)
  waiting for transfers between devices  8.95 us (6%)
  local copies, waits for them, and re-layouts  5.62 us (4%)
    pallas_call x1, Pallas kernels, near_field(): pl.pallas_call(near_kernel, out_shape=shape(rows, LANES), in_specs=[SMEM]...  42.7 us
    pallas_call x1, Pallas kernels, front(): pl.pallas_call(front_kernel, out_shape=(shape(devices, 2 * slots.shape[0]...  37.8 us
    pallas_call x1, Pallas kernels, back(): pl.pallas_call(back_kernel, out_shape=shape(rows, LANES), in_specs=[SMEM]...  28.7 us
    all_to_all x1, starting transfers between devices, exchange(): return lax.all_to_all(value, AXES, split_axis=0, concat_axis=0, tiled=True)  15.9 us
    all_to_all x1, waiting for transfers between devices, exchange(): return lax.all_to_all(value, AXES, split_axis=0, concat_axis=0, tiled=True)  8.94 us
    ppermute x2, starting transfers between devices, shift(): return lax.ppermute(value, AXES, pairs)  6.44 us
    unnamed x10, local copies, waits for them, and re-layouts  3.26 us
  transfers between devices with their start and end apart: 3, of which 1 were waited for; matrix products, arithmetic and copies ran while one was open for 2% of the time, Pallas kernels for 55%

profile of v3, /device:TPU:1, one launch (start us, length us, event | category | flops | bytes accessed | tf_op | source)
XLA Modules:
  0.0 146.8 jit_solution(8332022371852919650)
XLA Ops:
  0.0 0.9 slice.13
  0.9 1.1 copy.18
  2.0 0.0 copy-start.1
  2.0 4.5 %collective-permute-start = (f32[4,128]{1,0:T(4,128)S(1)}, f32[4,128]{1,0:T(4,128)S(1)}, u32[]{:S(2)}, u32[]{:S(2)}) collective-permute-start(f32[4,128]{1,0:T(4,128)S(1)} %bitcast.19), channel_id=1, source_target_pairs={{0,1},{1,2},{2,3},{3,4},{4,5},{5,6},{6,7},{7,8},{8,9},{9,10},{10,1... | collective-permute-start | bytes 6152 | tf_op jit(solution)/shard_map/ppermute | solution.py:494
  6.5 1.9 %collective-permute-start.1 = (f32[4,128]{1,0:T(4,128)S(1)}, f32[4,128]{1,0:T(4,128)S(1)}, u32[]{:S(2)}, u32[]{:S(2)}) collective-permute-start(f32[4,128]{1,0:T(4,128)S(1)} %bitcast.18), channel_id=1, source_target_pairs={{1,0},{2,1},{3,2},{4,3},{5,4},{6,5},{7,6},{8,7},{9,8},{10,9},{11,1... | collective-permute-start | bytes 6152 | tf_op jit(solution)/shard_map/ppermute | solution.py:494
  8.5 0.8 copy.14
  9.3 0.7 reshape.14.slots
  10.0 0.0 copy-done.1
  10.0 37.8 %front.1 = (f32[256,16,128]{2,1,0:T(8,128)}, bf16[128,256,128]{2,1,0:T(8,128)(2,1)}) custom-call(s32[2048]{0:T(1024)} %reshape.14.slots, s32[128]{0:T(128)} %classes.1, s32[128]{0:T(128)} %counts.3, s32[16384]{0:T(1024)} %targets.5, s32[16384]{0:T(1024)} %sources.5, f32[1,128]{1,0:T(1,128)} %constant.2.clone.signs, f32[3,256,128]{2,1,0:T(8,128)} %bitcast.10, ...), custom_call_target="tpu_custom_call" | custom-call | tf_op jit(solution)/shard_map/front/pallas_call | solution.py:412
  47.8 0.0 collective-permute-done.before
  47.8 0.0 copy-start.2
  47.8 0.0 collective-permute-done.1.after
  47.8 0.0 copy-start.3
  47.8 15.9 %all-to-all-start = ((f32[256,16,128]{2,1,0:T(8,128)}), f32[256,16,128]{2,1,0:T(8,128)S(1)}, u32[]{:S(2)}, u32[]{:S(2)}) async-start(f32[256,16,128]{2,1,0:T(8,128)} %get-tuple-element.14), calls=%async_computation | async-start | bytes 4194304 | tf_op jit(solution)/shard_map/all_to_all | solution.py:488
  63.7 0.7 reshape_reshape.3.slots
  65.1 0.0 copy-done.2
  65.1 0.0 copy-done.3
  65.1 42.7 %near_field.1.near = f32[256,128]{1,0:T(8,128)} custom-call(s32[4096]{0:T(1024)} %targets.4, s32[4096]{0:T(1024)} %sources.4, s32[1]{0:T(128)S(6)} %copy.19.count, f32[3,256,128]{2,1,0:T(8,128)} %bitcast.11, f32[256,128]{1,0:T(8,128)} %bitcast.15, f32[4,128]{1,0:T(4,128)} %copy-done.2, f32[4,128]{1,0:T(4,128)} %copy-done.3), custom_call_target="tpu_custom_call" | custom-call | tf_op jit(solution)/shard_map/near_field/pallas_call | solution.py:465
  107.8 8.9 %all-to-all-done.message = f32[256,16,128]{2,1,0:T(8,128)S(1)} async-done(((f32[256,16,128]{2,1,0:T(8,128)}), f32[256,16,128]{2,1,0:T(8,128)S(1)}, u32[]{:S(2)}, u32[]{:S(2)}) %all-to-all-start) | async-done | bytes 2097184 | tf_op jit(solution)/shard_map/all_to_all | solution.py:488
  116.7 0.0 copy-start
  116.7 1.4 copy-done
  118.1 28.7 %back.1 = f32[256,128]{1,0:T(8,128)} custom-call(s32[128]{0:T(128)} %counts.3, s32[16384]{0:T(1024)} %sources.5, s32[16384]{0:T(1024)} %targets.5, s32[8,256]{1,0:T(8,128)} %reshape_reshape.3.slots, f32[3,256,128]{2,1,0:T(8,128)} %bitcast.12, f32[256,128]{1,0:T(8,128)} %near_field.1.near, bf16[128,256,128]{2,1,0:T(8,128)(2,1)} %get-tuple-element.13.packed, ...), custom_call_target="tpu_custom_call" | custom-call | tf_op jit(solution)/shard_map/back/pallas_call | solution.py:440
  (2 shorter events, 0.0 us)
Async XLA Ops:
  2.0 8.0 %copy-start.1 = (f32[1,3,256,128]{3,2,1,0:T(8,128)}, f32[1,3,256,128]{3,2,1,0:T(8,128)S(1)}, u32[]{:S(2)}) copy-start(f32[1,3,256,128]{3,2,1,0:T(8,128)S(1)} %copy.18) | copy-start | bytes 1179652
  2.0 45.8 %collective-permute-start = (f32[4,128]{1,0:T(4,128)S(1)}, f32[4,128]{1,0:T(4,128)S(1)}, u32[]{:S(2)}, u32[]{:S(2)}) collective-permute-start(f32[4,128]{1,0:T(4,128)S(1)} %bitcast.19), channel_id=1, source_target_pairs={{0,1},{1,2},{2,3},{3,4},{4,5},{5,6},{6,7},{7,8},{8,9},{9,10},{10,1... | collective-permute-start | bytes 6152 | tf_op jit(solution)/shard_map/ppermute | solution.py:494
  6.5 41.3 %collective-permute-start.1 = (f32[4,128]{1,0:T(4,128)S(1)}, f32[4,128]{1,0:T(4,128)S(1)}, u32[]{:S(2)}, u32[]{:S(2)}) collective-permute-start(f32[4,128]{1,0:T(4,128)S(1)} %bitcast.18), channel_id=1, source_target_pairs={{1,0},{2,1},{3,2},{4,3},{5,4},{6,5},{7,6},{8,7},{9,8},{10,9},{11,1... | collective-permute-start | bytes 6152 | tf_op jit(solution)/shard_map/ppermute | solution.py:494
  47.8 17.3 %copy-start.2 = (f32[4,128]{1,0:T(4,128)}, f32[4,128]{1,0:T(4,128)S(1)}, u32[]{:S(2)}) copy-start(f32[4,128]{1,0:T(4,128)S(1)} %collective-permute-done.before) | copy-start | bytes 6148
  47.8 17.3 %copy-start.3 = (f32[4,128]{1,0:T(4,128)}, f32[4,128]{1,0:T(4,128)S(1)}, u32[]{:S(2)}) copy-start(f32[4,128]{1,0:T(4,128)S(1)} %collective-permute-done.1.after) | copy-start | bytes 6148
  47.8 68.9 %all-to-all-start = ((f32[256,16,128]{2,1,0:T(8,128)}), f32[256,16,128]{2,1,0:T(8,128)S(1)}, u32[]{:S(2)}, u32[]{:S(2)}) async-start(f32[256,16,128]{2,1,0:T(8,128)} %get-tuple-element.14), calls=%async_computation | async-start | bytes 4194304 | tf_op jit(solution)/shard_map/all_to_all | solution.py:488
  116.7 1.4 copy-start

commit v4 on v3

--- a/solution.py
+++ b/solution.py
@@ -16,7 +16,11 @@
 GROUP = 8
 ROWS = 16
 PAIRS = 32
-JOINT = 4
+JOINT = 8
+BESIDE = 32
+CAP = 8
+ROW_COUNT = 11
+SPARE = ROW_COUNT - CAP
 MIB = 1 << 20
 
 
@@ -61,6 +65,10 @@
             along_x = along_x * x
 
 
+def sum_sublanes(value, count):
+    return functools.reduce(lambda a, b: a + b, [value[pl.ds(i, count, GROUP), :] for i in range(GROUP)])
+
+
 def centred(turned, here):
     u = []
     for c in range(3):
@@ -69,6 +77,10 @@
     return u
 
 
+def block_of(here):
+    return here[1].start // LANES
+
+
 def blocks_of(rows):
     for half in range(2):
         for block in range(rows // LANES):
@@ -81,10 +93,10 @@
             groups[place + i] = n * size + i * ROWS
         return place + (counts[n] + ROWS - 1) // ROWS
 
-    return lax.fori_loop(0, batches, one, 0)
-
-
-def each_group(groups, number, step):
+    return lax.fori_loop(0, batches, one, 0, unroll=4)
+
+
+def each_group(groups, start, number, step):
     def several(turn, carry):
         step([groups[turn * JOINT + i] for i in range(JOINT)])
         return carry
@@ -93,15 +105,15 @@
         step([groups[turn]])
         return carry
 
-    lax.fori_loop(0, number // JOINT, several, 0)
-    lax.fori_loop(number // JOINT * JOINT, number, single, 0)
+    lax.fori_loop(start // JOINT, number // JOINT, several, 0)
+    lax.fori_loop(jnp.maximum(number // JOINT * JOINT, start), number, single, 0)
 
 
 def views(index, width):
     return [index.at[pl.ds(i, index.shape[0] - width + 1)] for i in range(width)]
 
 
-def gather_rows(groups, number, index, table, held):
+def gather_step(index, table, held):
     later = views(index, ROWS)
 
     def step(firsts):
@@ -110,7 +122,7 @@
             for i in range(ROWS):
                 held[pl.ds(first + i, 1), :] = rows[i]
 
-    each_group(groups, number, step)
+    return step
 
 
 def scatter_rows(groups, number, index, held, totals):
@@ -126,7 +138,7 @@
                 there = pl.ds(later[i][first], 1)
                 total[there, :] = total[there, :] + held[pl.ds(first + i, 1), :]
 
-    each_group(groups, number, step)
+    each_group(groups, 0, number, step)
 
 
 def sum_of(totals):
@@ -143,19 +155,24 @@
 
 
 def front_kernel(
-    slots, classes, counts, targets, sources, signs, pos, mass, operators,
-    message, packed,
-    turned, terms, table, rows, matrix, both, held, *rest,
+    slots, classes, counts, signs, pos, mass, operators, all_targets, all_sources,
+    message, groups, packed,
+    turned, terms, parts, table, rows, matrix, both, held, targets, sources, *rest,
 ):
-    *totals, groups, row_sem, out_sem = rest
+    *totals, row_sem, out_sem, target_sem, source_sem = rest
     batches = rows.shape[0]
     size = held.shape[0] // batches
     leaf_rows = mass.shape[0]
 
+    fetch_targets = pltpu.make_async_copy(all_targets, targets, target_sem)
+    fetch_targets.start()
+    fetch_sources = pltpu.make_async_copy(all_sources, sources, source_sem)
+    fetch_sources.start()
+
     def fetch(n):
         return pltpu.make_async_copy(operators.at[pl.ds(classes[n], 1), :], rows.at[pl.ds(n, 1), :], row_sem)
 
-    lax.fori_loop(0, batches, lambda n, c: (fetch(n).start(), c)[1], 0)
+    lax.fori_loop(0, batches, lambda n, c: (fetch(n).start(), c)[1], 0, unroll=8)
     for c in range(3):
         turned[c] = pos[c].T
     turned[3] = mass[...].T
@@ -163,27 +180,39 @@
     for half, here in blocks_of(leaf_rows):
 
         def visit(k, value, half=half, here=here):
-            terms[half, k : k + 1, here[1]] = jnp.sum(value, axis=0, keepdims=True)
+            whole = functools.reduce(lambda a, b: a + b, [value[i : i + GROUP] for i in range(0, LEAF, GROUP)])
+            parts[half, block_of(here), k * GROUP : (k + 1) * GROUP, :] = whole
 
         walk(*centred(turned, here), turned[(3,) + here], visit)
     for half in range(2):
+        for block in range(leaf_rows // LANES):
+            terms[half, :COEFFS, block * LANES : (block + 1) * LANES] = sum_sublanes(parts.at[half, block], COEFFS)
         table[pl.ds(half, leaf_rows, 2), :] = terms[half].T
-    cap = message.shape[1] // 2
-
+    devices = message.shape[0] // ROW_COUNT
     later = views(slots, ROWS)
 
     def export(group, carry):
         values = [table[pl.ds(later[i][group * ROWS], 1), :] for i in range(ROWS)]
         for i in range(ROWS):
-            message[group * (ROWS // cap) + i // cap, i % cap : i % cap + 1, :] = values[i]
-        return carry
-
-    lax.fori_loop(0, slots.shape[0] // ROWS, export, 0)
+            message[pl.ds(group * (ROWS // CAP * ROW_COUNT) + i // CAP * ROW_COUNT + i % CAP, 1), :] = values[i]
+        return carry
+
+    lax.fori_loop(0, slots.shape[0] // ROWS, export, 0, unroll=4)
     number = list_groups(counts, batches, size, groups)
-    gather_rows(groups, number, targets, table, held)
-    lax.fori_loop(0, batches, lambda n, c: (fetch(n).wait(), c)[1], 0)
+    groups[groups.shape[0] - 1] = number
+    fetch_targets.wait()
+    gather = gather_step(targets, table, held)
+    beside = BESIDE * batches // GROUP
+
+    def fill(place, carry):
+        groups[place] = 0
+        return carry
+
+    lax.fori_loop(number, beside, fill, 0)
+    lax.fori_loop(0, batches, lambda n, c: (fetch(n).wait(), c)[1], 0, unroll=8)
     lane = lane_id((GROUP, LANES))
     width = rows.shape[1]
+    flat = matrix.reshape(batches * LANES, LANES)
     matrix[:, COEFFS:, :] = jnp.zeros((batches, LANES - COEFFS, LANES), jnp.float32)
 
     def spread(group, carry):
@@ -202,10 +231,13 @@
                 value = jnp.where(lane < offset, part(first + 1), value)
             if offset:
                 value = pltpu.roll(value, LANES - offset, 1)
-            matrix[here, k, :] = jnp.where(lane < COEFFS, value, 0.0)
+            flat[pl.ds(group * GROUP * LANES + k, GROUP, LANES), :] = jnp.where(lane < COEFFS, value, 0.0)
+            if k * BESIDE // COEFFS < (k + 1) * BESIDE // COEFFS:
+                gather([groups[group * BESIDE + k * BESIDE // COEFFS]])
         return carry
 
     lax.fori_loop(0, batches // GROUP, spread, 0)
+    each_group(groups, beside, number, gather)
     row = lax.broadcasted_iota(jnp.int32, (size, LANES), 0)
 
     def product(n, carry):
@@ -220,8 +252,23 @@
     lax.fori_loop(0, batches, product, 0, unroll=8)
     save = pltpu.make_async_copy(both, packed, out_sem)
     save.start()
+    fetch_sources.wait()
     scatter_rows(groups, number, sources, held, totals)
-    message[:, cap:, :] = (sum_of(totals) * signs[...]).reshape(message.shape[0], cap, LANES)
+    totals[0][...] = sum_of(totals) * signs[...]
+    every = lane_id((devices, LANES))
+    holes = []
+    for c in range(CAP):
+        value = totals[0][pl.ds(c, devices, CAP), :]
+        if c < SPARE:
+            holes.append((CAP + c, value))
+        else:
+            first = 2 * (c - SPARE)
+            holes.append((first, jnp.where(every < COEFFS, 0.0, pltpu.roll(value, COEFFS, 1))))
+            holes.append((first + 1, jnp.where(every < COEFFS, 0.0, pltpu.roll(value, 2 * COEFFS - LANES, 1))))
+    for r in range(ROW_COUNT):
+        value = sum([v for place, v in holes if place == r], 0.0)
+        there = pl.ds(r, devices, ROW_COUNT)
+        message[there, :] = value if r >= CAP else message[there, :] + value
     save.wait()
 
 
@@ -285,7 +332,7 @@
                         source[leaf, (2 * pair_of + c) * 4 + q] = wide[first : first + GROUP, c * LANES : (c + 1) * LANES]
         return carry
 
-    lax.fori_loop(0, 3 * tiles, spread, 0, unroll=2)
+    lax.fori_loop(0, 3 * tiles, spread, 0, unroll=4)
 
     def spread_target(leaf, carry):
         for c in range(3):
@@ -325,32 +372,50 @@
     full = live // PAIRS
     lax.fori_loop(0, full, several, 0)
     lax.fori_loop(full * PAIRS, live, single, 0)
-    summed = jnp.sum(total[...], axis=1)
+    summed = sum_sublanes(total.reshape(2 * rows * GROUP, LANES), 2 * rows)
     ahead[0] = summed + pltpu.roll(summed, LEAF, 1)
     out[...] = -jnp.where(wide < LEAF, ahead[0, pl.ds(0, rows, 2), :], ahead[0, pl.ds(1, rows, 2), :])
 
 
 def back_kernel(
-    counts, sources, targets, slots, pos, near, packed, message,
+    counts, groups, slots, pos, near, packed, message, all_sources, all_targets,
     out,
-    table, returned, both, held, expansion, turned, terms, *rest,
+    rows_in, table, returned, both, held, expansion, turned, terms, sources, targets, *rest,
 ):
-    *totals, groups, matrix_sem, table_sem, returned_sem = rest
-    cap = table.shape[1]
+    *totals, matrix_sem, message_sem, source_sem, target_sem = rest
     batches = both.shape[0]
     size = held.shape[0] // batches
     rows = near.shape[0]
-    fetch_table = pltpu.make_async_copy(message.at[:, :cap, :], table, table_sem)
-    fetch_table.start()
-    fetch_returned = pltpu.make_async_copy(message.at[:, cap:, :], returned, returned_sem)
-    fetch_returned.start()
+    fetch_sources = pltpu.make_async_copy(all_sources, sources, source_sem)
+    fetch_sources.start()
+    fetch_message = pltpu.make_async_copy(message, rows_in, message_sem)
+    fetch_message.start()
+    fetch_targets = pltpu.make_async_copy(all_targets, targets, target_sem)
+    fetch_targets.start()
     fetch_matrix = pltpu.make_async_copy(packed, both, matrix_sem)
     fetch_matrix.start()
     for c in range(3):
         turned[c] = pos[c].T
-    number = list_groups(counts, batches, size, groups)
-    fetch_table.wait()
-    gather_rows(groups, number, sources, table.reshape(table.shape[0] * cap, LANES), held)
+    number = groups[groups.shape[0] - 1]
+    devices = rows_in.shape[0] // ROW_COUNT
+    every = lane_id((devices, LANES))
+    fetch_message.wait()
+
+    def received(r):
+        return rows_in[pl.ds(r, devices, ROW_COUNT), :]
+
+    for c in range(CAP):
+        table[pl.ds(c, devices, CAP), :] = received(c)
+        if c < SPARE:
+            value = received(CAP + c)
+        else:
+            first = 2 * (c - SPARE)
+            early = pltpu.roll(received(first), LANES - COEFFS, 1)
+            late = pltpu.roll(received(first + 1), 2 * (LANES - COEFFS), 1)
+            value = jnp.where(every < LANES - COEFFS, early, late)
+        returned[pl.ds(c, devices, CAP), :] = value
+    fetch_sources.wait()
+    each_group(groups, 0, number, gather_step(sources, table, held))
     fetch_matrix.wait()
     row = lax.broadcasted_iota(jnp.int32, (size, LANES), 0)
 
@@ -360,15 +425,14 @@
         return carry
 
     lax.fori_loop(0, batches, product, 0, unroll=8)
+    fetch_targets.wait()
     scatter_rows(groups, number, targets, held, totals)
-    fetch_returned.wait()
     chunk = slots.shape[1]
     leaf = lax.broadcasted_iota(jnp.int32, (expansion.shape[0], chunk), 0)
     sums = sum_of(totals)
     for block in range(slots.shape[0]):
         hot = (leaf == slots[block : block + 1, :]).astype(jnp.float32).astype(jnp.bfloat16)
-        part = returned[block * chunk // cap : (block + 1) * chunk // cap]
-        high, low = split(part.reshape(chunk, LANES))
+        high, low = split(returned[block * chunk : (block + 1) * chunk, :])
         sums = sums + jnp.dot(hot, high, preferred_element_type=jnp.float32)
         sums = sums + jnp.dot(hot, low, preferred_element_type=jnp.float32)
     expansion[...] = sums
@@ -402,61 +466,63 @@
     return pltpu.VMEM(dims, dtype)
 
 
-def group_list(pairs, batches):
-    return pltpu.SMEM((pairs // ROWS + pairs // batches // ROWS,), jnp.int32)
-
-
 def front(slots, classes, counts, targets, sources, pos, mass, operators, devices):
     rows = mass.shape[0]
     batches, pairs = classes.shape[0], targets.shape[0]
+    most = pairs // ROWS + pairs // batches // ROWS + 1
     return pl.pallas_call(
         front_kernel,
         out_shape=(
-            shape(devices, 2 * slots.shape[0] // devices, LANES),
+            shape(devices * ROW_COUNT, LANES),
+            jax.ShapeDtypeStruct((-(-most // 1024) * 1024,), jnp.int32),
             jax.ShapeDtypeStruct((batches, 2 * LANES, LANES), jnp.bfloat16),
         ),
-        in_specs=[SMEM] * 5 + [VMEM] * 3 + [ANY],
-        out_specs=(VMEM, ANY),
+        in_specs=[SMEM] * 3 + [VMEM] * 3 + [ANY] * 3,
+        out_specs=(VMEM, SMEM, ANY),
         scratch_shapes=[
             scratch(4, LANES, rows),
             scratch(2, LANES, rows),
+            scratch(2, rows // LANES, COEFFS * GROUP, LANES),
             scratch(2 * rows, LANES),
             scratch(batches, operators.shape[1]),
             scratch(batches, LANES, LANES),
             scratch(batches, 2 * LANES, LANES, dtype=jnp.bfloat16),
             scratch(pairs, LANES),
+            pltpu.SMEM((pairs,), jnp.int32),
+            pltpu.SMEM((pairs,), jnp.int32),
         ]
         + [scratch(slots.shape[0], LANES)] * ACCS
-        + [group_list(pairs, batches)]
-        + [pltpu.SemaphoreType.DMA] * 2,
+        + [pltpu.SemaphoreType.DMA] * 4,
         compiler_params=params(58),
         name="front",
-    )(slots, classes, counts, targets, sources, jnp.asarray(SIGNS), pos, mass, operators)
-
-
-def back(counts, sources, targets, slots, pos, near, packed, message):
+    )(slots, classes, counts, jnp.asarray(SIGNS), pos, mass, operators, targets, sources)
+
+
+def back(counts, groups, sources, targets, slots, pos, near, packed, message):
     rows = near.shape[0]
-    cap = message.shape[1] // 2
+    pairs = sources.shape[0]
     return pl.pallas_call(
         back_kernel,
         out_shape=shape(rows, LANES),
-        in_specs=[SMEM] * 3 + [VMEM] * 3 + [ANY] * 2,
+        in_specs=[SMEM] * 2 + [VMEM] * 3 + [ANY] * 4,
         out_specs=VMEM,
         scratch_shapes=[
-            scratch(message.shape[0], cap, LANES),
-            scratch(message.shape[0], cap, LANES),
+            scratch(*message.shape),
+            scratch(slots.size, LANES),
+            scratch(slots.size, LANES),
             scratch(*packed.shape, dtype=jnp.bfloat16),
-            scratch(sources.shape[0], LANES),
+            scratch(pairs, LANES),
             scratch(2 * rows, LANES),
             scratch(4, LANES, rows),
             scratch(2, LANES, rows),
+            pltpu.SMEM((pairs,), jnp.int32),
+            pltpu.SMEM((pairs,), jnp.int32),
         ]
         + [scratch(2 * rows, LANES)] * ACCS
-        + [group_list(sources.shape[0], counts.shape[0])]
-        + [pltpu.SemaphoreType.DMA] * 3,
+        + [pltpu.SemaphoreType.DMA] * 4,
         compiler_params=params(58),
         name="back",
-    )(counts, sources, targets, slots, pos, near, packed, message)
+    )(counts, groups, slots, pos, near, packed, message, sources, targets)
 
 
 def near_field(targets, sources, count, pos, mass, before, after):
@@ -485,7 +551,9 @@
 
 
 def exchange(value):
-    return lax.all_to_all(value, AXES, split_axis=0, concat_axis=0, tiled=True)
+    devices = lax.axis_size("group") * lax.axis_size("dom")
+    blocks = value.reshape(devices, -1, 1, LANES)
+    return lax.all_to_all(blocks, AXES, split_axis=0, concat_axis=0, tiled=True).reshape(value.shape)
 
 
 def shift(value, forward):
@@ -514,11 +582,11 @@
     ends = jnp.concatenate([pos[:, :: mass.shape[0] - 1], mass[None, :: mass.shape[0] - 1]], axis=0)
     before = shift(ends[:, 1], True)
     after = shift(ends[:, 0], False)
-    message, packed = front(slots, far_class, far_count, far_target, far_source, pos, mass, operators, devices)
+    message, groups, packed = front(slots, far_class, far_count, far_target, far_source, pos, mass, operators, devices)
     message, before, after = lax.optimization_barrier((message, before, after))
     message = exchange(message)
     near = near_field(near_target, near_source, near_count, pos, mass, before, after)
-    out = back(far_count, far_source, far_target, slots.reshape(8, -1), pos, near, packed, message)
+    out = back(far_count, groups, far_source, far_target, slots.reshape(8, -1), pos, near, packed, message)
     return out.reshape(-1)
 
 

time: 148 us -> 135 us (0.912)
  the two profiles are of different devices: /device:TPU:1 before, /device:TPU:56 now
where the time goes in v4:
time: 135 us
  Pallas kernels  109 us (81%)
  starting transfers between devices  19.8 us (15%)
  local copies, waits for them, and re-layouts  5.45 us (4%)
    pallas_call x1, Pallas kernels, near_field(): pl.pallas_call(near_kernel, out_shape=shape(rows, LANES), in_specs=[SMEM]...  45.3 us
    pallas_call x1, Pallas kernels, front(): pl.pallas_call(front_kernel, out_shape=(shape(devices * ROW_COUNT, LANES)...  34.4 us
    pallas_call x1, Pallas kernels, back(): pl.pallas_call(back_kernel, out_shape=shape(rows, LANES), in_specs=[SMEM]...  28.9 us
    all_to_all x1, starting transfers between devices, exchange(): lax.all_to_all(blocks, AXES, split_axis=0, concat_axis=0, tiled=True)  12.2 us
    ppermute x2, starting transfers between devices, shift(): return lax.ppermute(value, AXES, pairs)  7.67 us
    unnamed x10, local copies, waits for them, and re-layouts  3.08 us
  transfers between devices with their start and end apart: 3, of which 0 were waited for; matrix products, arithmetic and copies ran while one was open for 2% of the time, Pallas kernels for 59%

profile of v4, /device:TPU:56, one launch (start us, length us, event | category | flops | bytes accessed | tf_op | source)
XLA Modules:
  0.0 134.8 jit_solution(14412531416940853389)
XLA Ops:
  0.0 0.9 slice.13
  0.9 1.1 copy.21
  2.0 0.0 copy-start
  2.0 1.9 %collective-permute-start = (f32[4,128]{1,0:T(4,128)S(1)}, f32[4,128]{1,0:T(4,128)S(1)}, u32[]{:S(2)}, u32[]{:S(2)}) collective-permute-start(f32[4,128]{1,0:T(4,128)S(1)} %bitcast.23), channel_id=1, source_target_pairs={{0,1},{1,2},{2,3},{3,4},{4,5},{5,6},{6,7},{7,8},{8,9},{9,10},{10,1... | collective-permute-start | bytes 6152 | tf_op jit(solution)/shard_map/ppermute | solution.py:562
  4.0 5.8 %collective-permute-start.1 = (f32[4,128]{1,0:T(4,128)S(1)}, f32[4,128]{1,0:T(4,128)S(1)}, u32[]{:S(2)}, u32[]{:S(2)}) collective-permute-start(f32[4,128]{1,0:T(4,128)S(1)} %bitcast.22), channel_id=1, source_target_pairs={{1,0},{2,1},{3,2},{4,3},{5,4},{6,5},{7,6},{8,7},{9,8},{10,9},{11,1... | collective-permute-start | bytes 6152 | tf_op jit(solution)/shard_map/ppermute | solution.py:562
  9.7 0.8 copy.16
  10.5 0.7 reshape.18.slots
  11.3 0.0 copy-done
  11.3 34.4 %front.1 = (f32[2816,128]{1,0:T(8,128)}, s32[2048]{0:T(1024)}, bf16[128,256,128]{2,1,0:T(8,128)(2,1)}) custom-call(s32[2048]{0:T(1024)} %reshape.18.slots, s32[128]{0:T(128)} %classes.1, s32[128]{0:T(128)} %counts.3, f32[1,128]{1,0:T(1,128)} %constant.2.clone.signs, f32[3,256,128]{2,1,0:T(8,128)} %bitcast.12, f32[256,128]{1,0:T(8,128)} %bitcast.18, ...), custom_call_target="tpu_custom_call" | custom-call | tf_op jit(solution)/shard_map/front/pallas_call | solution.py:473
  45.7 0.0 collective-permute-done.before
  45.7 0.0 copy-start.2
  45.7 0.0 collective-permute-done.1.after
  45.7 0.0 copy-start.3
  45.7 12.2 %all-to-all-start = ((f32[256,11,1,128]{3,2,1,0:T(1,128)}), f32[256,11,1,128]{3,2,1,0:T(1,128)S(1)}, u32[]{:S(2)}, u32[]{:S(2)}) async-start(f32[256,11,1,128]{3,2,1,0:T(1,128)} %bitcast.16), calls=%async_computation | async-start | bytes 2883584 | tf_op jit(solution)/shard_map/all_to_all | solution.py:556
  57.9 0.7 reshape_reshape.3.slots
  59.2 0.0 copy-done.2
  59.2 0.0 copy-done.3
  59.3 45.3 %near_field.1.near = f32[256,128]{1,0:T(8,128)} custom-call(s32[4096]{0:T(1024)} %targets.1, s32[4096]{0:T(1024)} %sources.1, s32[1]{0:T(128)S(6)} %copy.22.count, f32[3,256,128]{2,1,0:T(8,128)} %bitcast.13, f32[256,128]{1,0:T(8,128)} %bitcast.19, f32[4,128]{1,0:T(4,128)} %copy-done.2, f32[4,128]{1,0:T(4,128)} %copy-done.3), custom_call_target="tpu_custom_call" | custom-call | tf_op jit(solution)/shard_map/near_field/pallas_call | solution.py:531
  104.5 0.0 all-to-all-done
  104.5 0.0 copy-start.1
  104.5 1.2 copy-done.1
  105.7 28.9 %back.1 = f32[256,128]{1,0:T(8,128)} custom-call(s32[128]{0:T(128)} %counts.3, s32[2048]{0:T(1024)} %get-tuple-element.11.groups, s32[8,256]{1,0:T(8,128)} %reshape_reshape.3.slots, f32[3,256,128]{2,1,0:T(8,128)} %bitcast.14, f32[256,128]{1,0:T(8,128)} %near_field.1.near, bf16[128,256,128]{2,1,0:T(8,128)(2,1)} %get-tuple-element.15.packed, ...), custom_call_target="tpu_custom_call" | custom-call | tf_op jit(solution)/shard_map/back/pallas_call | solution.py:504
  (2 shorter events, 0.0 us)
Async XLA Ops:
  2.0 9.3 %copy-start = (f32[1,3,256,128]{3,2,1,0:T(8,128)}, f32[1,3,256,128]{3,2,1,0:T(8,128)S(1)}, u32[]{:S(2)}) copy-start(f32[1,3,256,128]{3,2,1,0:T(8,128)S(1)} %copy.21) | copy-start | bytes 1179652
  2.0 43.6 %collective-permute-start = (f32[4,128]{1,0:T(4,128)S(1)}, f32[4,128]{1,0:T(4,128)S(1)}, u32[]{:S(2)}, u32[]{:S(2)}) collective-permute-start(f32[4,128]{1,0:T(4,128)S(1)} %bitcast.23), channel_id=1, source_target_pairs={{0,1},{1,2},{2,3},{3,4},{4,5},{5,6},{6,7},{7,8},{8,9},{9,10},{10,1... | collective-permute-start | bytes 6152 | tf_op jit(solution)/shard_map/ppermute | solution.py:562
  4.0 41.7 %collective-permute-start.1 = (f32[4,128]{1,0:T(4,128)S(1)}, f32[4,128]{1,0:T(4,128)S(1)}, u32[]{:S(2)}, u32[]{:S(2)}) collective-permute-start(f32[4,128]{1,0:T(4,128)S(1)} %bitcast.22), channel_id=1, source_target_pairs={{1,0},{2,1},{3,2},{4,3},{5,4},{6,5},{7,6},{8,7},{9,8},{10,9},{11,1... | collective-permute-start | bytes 6152 | tf_op jit(solution)/shard_map/ppermute | solution.py:562
  45.7 13.6 %copy-start.2 = (f32[4,128]{1,0:T(4,128)}, f32[4,128]{1,0:T(4,128)S(1)}, u32[]{:S(2)}) copy-start(f32[4,128]{1,0:T(4,128)S(1)} %collective-permute-done.before) | copy-start | bytes 6148
  45.7 13.5 %copy-start.3 = (f32[4,128]{1,0:T(4,128)}, f32[4,128]{1,0:T(4,128)S(1)}, u32[]{:S(2)}) copy-start(f32[4,128]{1,0:T(4,128)S(1)} %collective-permute-done.1.after) | copy-start | bytes 6148
  45.7 58.8 %all-to-all-start = ((f32[256,11,1,128]{3,2,1,0:T(1,128)}), f32[256,11,1,128]{3,2,1,0:T(1,128)S(1)}, u32[]{:S(2)}, u32[]{:S(2)}) async-start(f32[256,11,1,128]{3,2,1,0:T(1,128)} %bitcast.16), calls=%async_computation | async-start | bytes 2883584 | tf_op jit(solution)/shard_map/all_to_all | solution.py:556
  104.5 1.2 copy-start.1

commit v5 on v4

--- a/solution.py
+++ b/solution.py
@@ -15,8 +15,8 @@
 ACCS = 8
 GROUP = 8
 ROWS = 16
-PAIRS = 32
-JOINT = 8
+PAIRS = 64
+JOINT = 4
 BESIDE = 32
 CAP = 8
 ROW_COUNT = 11
@@ -88,9 +88,12 @@
 
 
 def list_groups(counts, batches, size, groups):
+    share = size // ROWS
+    later = [groups.at[pl.ds(i, groups.shape[0] - share + 1)] for i in range(share)]
+
     def one(n, place):
-        for i in range(size // ROWS):
-            groups[place + i] = n * size + i * ROWS
+        for i in range(share):
+            later[i][place] = n * size + i * ROWS
         return place + (counts[n] + ROWS - 1) // ROWS
 
     return lax.fori_loop(0, batches, one, 0, unroll=4)
@@ -155,15 +158,17 @@
 
 
 def front_kernel(
-    slots, classes, counts, signs, pos, mass, operators, all_targets, all_sources,
+    classes, counts, signs, pos, mass, operators, all_slots, all_targets, all_sources,
     message, groups, packed,
-    turned, terms, parts, table, rows, matrix, both, held, targets, sources, *rest,
+    turned, terms, parts, table, rows, matrix, both, held, slots, targets, sources, *rest,
 ):
-    *totals, row_sem, out_sem, target_sem, source_sem = rest
+    *totals, row_sem, out_sem, slot_sem, target_sem, source_sem = rest
     batches = rows.shape[0]
     size = held.shape[0] // batches
     leaf_rows = mass.shape[0]
 
+    fetch_slots = pltpu.make_async_copy(all_slots, slots, slot_sem)
+    fetch_slots.start()
     fetch_targets = pltpu.make_async_copy(all_targets, targets, target_sem)
     fetch_targets.start()
     fetch_sources = pltpu.make_async_copy(all_sources, sources, source_sem)
@@ -189,15 +194,15 @@
             terms[half, :COEFFS, block * LANES : (block + 1) * LANES] = sum_sublanes(parts.at[half, block], COEFFS)
         table[pl.ds(half, leaf_rows, 2), :] = terms[half].T
     devices = message.shape[0] // ROW_COUNT
-    later = views(slots, ROWS)
-
-    def export(group, carry):
-        values = [table[pl.ds(later[i][group * ROWS], 1), :] for i in range(ROWS)]
-        for i in range(ROWS):
-            message[pl.ds(group * (ROWS // CAP * ROW_COUNT) + i // CAP * ROW_COUNT + i % CAP, 1), :] = values[i]
-        return carry
-
-    lax.fori_loop(0, slots.shape[0] // ROWS, export, 0, unroll=4)
+    fetch_slots.wait()
+
+    def export(device, carry):
+        values = [table[pl.ds(slots[c, device], 1), :] for c in range(CAP)]
+        for c in range(CAP):
+            message[pl.ds(device * ROW_COUNT + c, 1), :] = values[c]
+        return carry
+
+    lax.fori_loop(0, devices, export, 0, unroll=8)
     number = list_groups(counts, batches, size, groups)
     groups[groups.shape[0] - 1] = number
     fetch_targets.wait()
@@ -249,7 +254,7 @@
         held[here, :] = multiply(value, jnp.concatenate([high, low], axis=0))
         return carry
 
-    lax.fori_loop(0, batches, product, 0, unroll=8)
+    lax.fori_loop(0, batches, product, 0, unroll=16)
     save = pltpu.make_async_copy(both, packed, out_sem)
     save.start()
     fetch_sources.wait()
@@ -272,7 +277,15 @@
     save.wait()
 
 
-def near_kernel(targets, sources, count, pos, mass, before, after, out, extended, lines, choose, ahead, source, target, total):
+def near_kernel(
+    count, pos, mass, before, after, all_targets, all_sources,
+    out,
+    extended, lines, choose, ahead, source, target, total, targets, sources, target_sem, source_sem,
+):
+    fetch_targets = pltpu.make_async_copy(all_targets, targets, target_sem)
+    fetch_targets.start()
+    fetch_sources = pltpu.make_async_copy(all_sources, sources, source_sem)
+    fetch_sources.start()
     rows = mass.shape[0]
     wide = lane_id((rows, LANES))
     for c in range(4):
@@ -363,33 +376,33 @@
             total[here] = total[here] + value
         return carry
 
-    def single(j, carry):
-        here, value = pair(targets[j], sources[j])
-        total[here] = total[here] + value
-        return carry
-
+    fetch_targets.wait()
+    fetch_sources.wait()
     live = count[0]
-    full = live // PAIRS
-    lax.fori_loop(0, full, several, 0)
-    lax.fori_loop(full * PAIRS, live, single, 0)
+    turns = (live + PAIRS - 1) // PAIRS
+
+    def fill(j, carry):
+        sources[j] = source.shape[0] - 1
+        return carry
+
+    lax.fori_loop(live, turns * PAIRS, fill, 0)
+    lax.fori_loop(0, turns, several, 0)
     summed = sum_sublanes(total.reshape(2 * rows * GROUP, LANES), 2 * rows)
     ahead[0] = summed + pltpu.roll(summed, LEAF, 1)
     out[...] = -jnp.where(wide < LEAF, ahead[0, pl.ds(0, rows, 2), :], ahead[0, pl.ds(1, rows, 2), :])
 
 
 def back_kernel(
-    counts, groups, slots, pos, near, packed, message, all_sources, all_targets,
+    counts, groups, slots, pos, near, rows_in, packed, all_sources, all_targets,
     out,
-    rows_in, table, returned, both, held, expansion, turned, terms, sources, targets, *rest,
+    table, returned, both, held, expansion, turned, terms, sources, targets, *rest,
 ):
-    *totals, matrix_sem, message_sem, source_sem, target_sem = rest
+    *totals, matrix_sem, source_sem, target_sem = rest
     batches = both.shape[0]
     size = held.shape[0] // batches
     rows = near.shape[0]
     fetch_sources = pltpu.make_async_copy(all_sources, sources, source_sem)
     fetch_sources.start()
-    fetch_message = pltpu.make_async_copy(message, rows_in, message_sem)
-    fetch_message.start()
     fetch_targets = pltpu.make_async_copy(all_targets, targets, target_sem)
     fetch_targets.start()
     fetch_matrix = pltpu.make_async_copy(packed, both, matrix_sem)
@@ -399,7 +412,6 @@
     number = groups[groups.shape[0] - 1]
     devices = rows_in.shape[0] // ROW_COUNT
     every = lane_id((devices, LANES))
-    fetch_message.wait()
 
     def received(r):
         return rows_in[pl.ds(r, devices, ROW_COUNT), :]
@@ -413,7 +425,7 @@
             early = pltpu.roll(received(first), LANES - COEFFS, 1)
             late = pltpu.roll(received(first + 1), 2 * (LANES - COEFFS), 1)
             value = jnp.where(every < LANES - COEFFS, early, late)
-        returned[pl.ds(c, devices, CAP), :] = value
+        returned[c * devices : (c + 1) * devices, :] = value
     fetch_sources.wait()
     each_group(groups, 0, number, gather_step(sources, table, held))
     fetch_matrix.wait()
@@ -424,7 +436,7 @@
         held[here, :] = multiply(jnp.where(row < counts[n], held[here, :], 0.0), both[n])
         return carry
 
-    lax.fori_loop(0, batches, product, 0, unroll=8)
+    lax.fori_loop(0, batches, product, 0, unroll=16)
     fetch_targets.wait()
     scatter_rows(groups, number, targets, held, totals)
     chunk = slots.shape[1]
@@ -477,7 +489,7 @@
             jax.ShapeDtypeStruct((-(-most // 1024) * 1024,), jnp.int32),
             jax.ShapeDtypeStruct((batches, 2 * LANES, LANES), jnp.bfloat16),
         ),
-        in_specs=[SMEM] * 3 + [VMEM] * 3 + [ANY] * 3,
+        in_specs=[SMEM] * 2 + [VMEM] * 3 + [ANY] * 4,
         out_specs=(VMEM, SMEM, ANY),
         scratch_shapes=[
             scratch(4, LANES, rows),
@@ -488,14 +500,15 @@
             scratch(batches, LANES, LANES),
             scratch(batches, 2 * LANES, LANES, dtype=jnp.bfloat16),
             scratch(pairs, LANES),
+            pltpu.SMEM(slots.shape, jnp.int32),
             pltpu.SMEM((pairs,), jnp.int32),
             pltpu.SMEM((pairs,), jnp.int32),
         ]
-        + [scratch(slots.shape[0], LANES)] * ACCS
-        + [pltpu.SemaphoreType.DMA] * 4,
+        + [scratch(slots.size, LANES)] * ACCS
+        + [pltpu.SemaphoreType.DMA] * 5,
         compiler_params=params(58),
         name="front",
-    )(slots, classes, counts, jnp.asarray(SIGNS), pos, mass, operators, targets, sources)
+    )(classes, counts, jnp.asarray(SIGNS), pos, mass, operators, slots, targets, sources)
 
 
 def back(counts, groups, sources, targets, slots, pos, near, packed, message):
@@ -504,10 +517,9 @@
     return pl.pallas_call(
         back_kernel,
         out_shape=shape(rows, LANES),
-        in_specs=[SMEM] * 2 + [VMEM] * 3 + [ANY] * 4,
+        in_specs=[SMEM] * 2 + [VMEM] * 4 + [ANY] * 3,
         out_specs=VMEM,
         scratch_shapes=[
-            scratch(*message.shape),
             scratch(slots.size, LANES),
             scratch(slots.size, LANES),
             scratch(*packed.shape, dtype=jnp.bfloat16),
@@ -519,10 +531,10 @@
             pltpu.SMEM((pairs,), jnp.int32),
         ]
         + [scratch(2 * rows, LANES)] * ACCS
-        + [pltpu.SemaphoreType.DMA] * 4,
-        compiler_params=params(58),
+        + [pltpu.SemaphoreType.DMA] * 3,
+        compiler_params=params(62),
         name="back",
-    )(counts, groups, slots, pos, near, packed, message, sources, targets)
+    )(counts, groups, slots, pos, near, message, packed, sources, targets)
 
 
 def near_field(targets, sources, count, pos, mass, before, after):
@@ -531,7 +543,7 @@
     return pl.pallas_call(
         near_kernel,
         out_shape=shape(rows, LANES),
-        in_specs=[SMEM] * 3 + [VMEM] * 4,
+        in_specs=[SMEM] + [VMEM] * 4 + [ANY] * 2,
         out_specs=VMEM,
         scratch_shapes=[
             scratch(4, blocks * GROUP, LANES),
@@ -541,10 +553,14 @@
             scratch(2 * blocks * GROUP, 16, GROUP, LANES),
             scratch(2 * rows, 3, GROUP, LANES),
             scratch(2 * rows, GROUP, LANES),
+            pltpu.SMEM(targets.shape, jnp.int32),
+            pltpu.SMEM(sources.shape, jnp.int32),
+            pltpu.SemaphoreType.DMA,
+            pltpu.SemaphoreType.DMA,
         ],
         compiler_params=params(58),
         name="near_field",
-    )(targets, sources, count, pos, mass, before, after)
+    )(count, pos, mass, before, after, targets, sources)
 
 
 AXES = ("group", "dom")
@@ -576,7 +592,7 @@
     operators,
 ):
     devices = lax.axis_size("group") * lax.axis_size("dom")
-    slots = export_slots.reshape(-1)
+    slots = export_slots.T
     pos = positions.reshape(3, -1, LANES)
     mass = masses.reshape(-1, LANES)
     ends = jnp.concatenate([pos[:, :: mass.shape[0] - 1], mass[None, :: mass.shape[0] - 1]], axis=0)
@@ -586,7 +602,7 @@
     message, before, after = lax.optimization_barrier((message, before, after))
     message = exchange(message)
     near = near_field(near_target, near_source, near_count, pos, mass, before, after)
-    out = back(far_count, groups, far_source, far_target, slots.reshape(8, -1), pos, near, packed, message)
+    out = back(far_count, groups, far_source, far_target, slots, pos, near, packed, message)
     return out.reshape(-1)
 
 

time: 135 us -> 129 us (0.956)
  the two profiles are of different devices: /device:TPU:56 before, /device:TPU:79 now
where the time goes in v5:
time: 129 us
  Pallas kernels  105 us (81%)
  starting transfers between devices  19.9 us (15%)
  local copies, waits for them, and re-layouts  3.2 us (2%)
    pallas_call x1, Pallas kernels, near_field(): pl.pallas_call(near_kernel, out_shape=shape(rows, LANES), in_specs=[SMEM]...  44.9 us
    pallas_call x1, Pallas kernels, front(): pl.pallas_call(front_kernel, out_shape=(shape(devices * ROW_COUNT, LANES)...  33.8 us
    pallas_call x1, Pallas kernels, back(): pl.pallas_call(back_kernel, out_shape=shape(rows, LANES), in_specs=[SMEM]...  26.5 us
    all_to_all x1, starting transfers between devices, exchange(): lax.all_to_all(blocks, AXES, split_axis=0, concat_axis=0, tiled=True)  14.3 us
    ppermute x2, starting transfers between devices, shift(): return lax.ppermute(value, AXES, pairs)  5.6 us
  transfers between devices with their start and end apart: 3, of which 0 were waited for; matrix products, arithmetic and copies ran while one was open for 0% of the time, Pallas kernels for 61%

profile of v5, /device:TPU:79, one launch (start us, length us, event | category | flops | bytes accessed | tf_op | source)
XLA Modules:
  0.0 129.2 jit_solution(17555933815724506650)
XLA Ops:
  0.0 0.9 slice.13
  0.9 1.1 copy.16
  2.0 0.0 copy-start
  2.0 3.7 %collective-permute-start = (f32[4,128]{1,0:T(4,128)S(1)}, f32[4,128]{1,0:T(4,128)S(1)}, u32[]{:S(2)}, u32[]{:S(2)}) collective-permute-start(f32[4,128]{1,0:T(4,128)S(1)} %bitcast.26), channel_id=1, source_target_pairs={{0,1},{1,2},{2,3},{3,4},{4,5},{5,6},{6,7},{7,8},{8,9},{9,10},{10,1... | collective-permute-start | bytes 6152 | tf_op jit(solution)/shard_map/ppermute | solution.py:578
  5.7 1.9 %collective-permute-start.1 = (f32[4,128]{1,0:T(4,128)S(1)}, f32[4,128]{1,0:T(4,128)S(1)}, u32[]{:S(2)}, u32[]{:S(2)}) collective-permute-start(f32[4,128]{1,0:T(4,128)S(1)} %bitcast.25), channel_id=1, source_target_pairs={{1,0},{2,1},{3,2},{4,3},{5,4},{6,5},{7,6},{8,7},{9,8},{10,9},{11,1... | collective-permute-start | bytes 6152 | tf_op jit(solution)/shard_map/ppermute | solution.py:578
  7.6 0.0 copy-done
  7.7 33.8 %front.1 = (f32[2816,128]{1,0:T(8,128)}, s32[2048]{0:T(1024)}, bf16[128,256,128]{2,1,0:T(8,128)(2,1)}) custom-call(s32[128]{0:T(128)} %classes.1, s32[128]{0:T(128)} %counts.3, f32[1,128]{1,0:T(1,128)} %constant.2.clone.signs, f32[3,256,128]{2,1,0:T(8,128)} %bitcast.13, f32[256,128]{1,0:T(8,128)} %bitcast.19, f32[316,7056]{1,0:T(8,128)} %operators.1, ...), custom_call_target="tpu_custom_call" | custom-call | tf_op jit(solution)/shard_map/front/pallas_call | solution.py:485
  41.4 0.0 collective-permute-done.before
  41.4 0.0 copy-start.2
  41.4 0.0 collective-permute-done.1.after
  41.5 0.0 copy-start.3
  41.5 14.3 %all-to-all-start = ((f32[256,11,1,128]{3,2,1,0:T(1,128)}), f32[256,11,1,128]{3,2,1,0:T(1,128)S(1)}, u32[]{:S(2)}, u32[]{:S(2)}) async-start(f32[256,11,1,128]{3,2,1,0:T(1,128)} %bitcast.17), calls=%async_computation | async-start | bytes 2883584 | tf_op jit(solution)/shard_map/all_to_all | solution.py:572
  56.4 0.0 copy-done.2
  56.4 0.0 copy-done.3
  56.4 44.9 %near_field.1.near = f32[256,128]{1,0:T(8,128)} custom-call(s32[1]{0:T(128)S(6)} %copy.17.count, f32[3,256,128]{2,1,0:T(8,128)} %bitcast.14, f32[256,128]{1,0:T(8,128)} %bitcast.20, f32[4,128]{1,0:T(4,128)} %copy-done.2, f32[4,128]{1,0:T(4,128)} %copy-done.3, s32[4096]{0:T(1024)} %all_targets.4, s32[4096]{0:T(1024)} %all_sources.4), custom_call_target="tpu_custom_call" | custom-call | tf_op jit(solution)/shard_map/near_field/pallas_call | solution.py:543
  101.3 0.0 all-to-all-done
  101.3 0.0 copy-start.1
  101.3 1.2 copy-done.1
  102.5 26.5 %back.1 = f32[256,128]{1,0:T(8,128)} custom-call(s32[128]{0:T(128)} %counts.3, s32[2048]{0:T(1024)} %get-tuple-element.11.groups, s32[8,256]{1,0:T(8,128)} %bitcast.23, f32[3,256,128]{2,1,0:T(8,128)} %bitcast.15, f32[256,128]{1,0:T(8,128)} %near_field.1.near, f32[2816,128]{1,0:T(8,128)} %bitcast.16, bf16[128,256,128]{2,1,0:T(8,128)(2,1)} %get-tuple-element.16.packed, ...), custom_call_target="tpu_custom_call" | custom-call | tf_op jit(solution)/shard_map/back/pallas_call | solution.py:517
  (2 shorter events, 0.0 us)
Async XLA Ops:
  2.0 5.7 %copy-start = (f32[1,3,256,128]{3,2,1,0:T(8,128)}, f32[1,3,256,128]{3,2,1,0:T(8,128)S(1)}, u32[]{:S(2)}) copy-start(f32[1,3,256,128]{3,2,1,0:T(8,128)S(1)} %copy.16) | copy-start | bytes 1179652
  2.0 39.4 %collective-permute-start = (f32[4,128]{1,0:T(4,128)S(1)}, f32[4,128]{1,0:T(4,128)S(1)}, u32[]{:S(2)}, u32[]{:S(2)}) collective-permute-start(f32[4,128]{1,0:T(4,128)S(1)} %bitcast.26), channel_id=1, source_target_pairs={{0,1},{1,2},{2,3},{3,4},{4,5},{5,6},{6,7},{7,8},{8,9},{9,10},{10,1... | collective-permute-start | bytes 6152 | tf_op jit(solution)/shard_map/ppermute | solution.py:578
  5.7 35.7 %collective-permute-start.1 = (f32[4,128]{1,0:T(4,128)S(1)}, f32[4,128]{1,0:T(4,128)S(1)}, u32[]{:S(2)}, u32[]{:S(2)}) collective-permute-start(f32[4,128]{1,0:T(4,128)S(1)} %bitcast.25), channel_id=1, source_target_pairs={{1,0},{2,1},{3,2},{4,3},{5,4},{6,5},{7,6},{8,7},{9,8},{10,9},{11,1... | collective-permute-start | bytes 6152 | tf_op jit(solution)/shard_map/ppermute | solution.py:578
  41.4 15.0 %copy-start.2 = (f32[4,128]{1,0:T(4,128)}, f32[4,128]{1,0:T(4,128)S(1)}, u32[]{:S(2)}) copy-start(f32[4,128]{1,0:T(4,128)S(1)} %collective-permute-done.before) | copy-start | bytes 6148
  41.5 14.9 %copy-start.3 = (f32[4,128]{1,0:T(4,128)}, f32[4,128]{1,0:T(4,128)S(1)}, u32[]{:S(2)}) copy-start(f32[4,128]{1,0:T(4,128)S(1)} %collective-permute-done.1.after) | copy-start | bytes 6148
  41.5 59.9 %all-to-all-start = ((f32[256,11,1,128]{3,2,1,0:T(1,128)}), f32[256,11,1,128]{3,2,1,0:T(1,128)S(1)}, u32[]{:S(2)}, u32[]{:S(2)}) async-start(f32[256,11,1,128]{3,2,1,0:T(1,128)} %bitcast.17), calls=%async_computation | async-start | bytes 2883584 | tf_op jit(solution)/shard_map/all_to_all | solution.py:572
  101.3 1.2 copy-start.1

commit v6 on v5

--- a/solution.py
+++ b/solution.py
@@ -154,7 +154,12 @@
 
 def multiply(value, both):
     high, low = split(value)
-    return dot(high, both[:LANES]) + dot(low, both[:LANES]) + dot(high, both[LANES:])
+    upper, lower = both[:LANES], both[LANES:]
+    square = jnp.concatenate(
+        [jnp.concatenate([upper, lower], axis=1), jnp.concatenate([upper, jnp.zeros_like(lower)], axis=1)], axis=0
+    )
+    wide = dot(jnp.concatenate([high, low], axis=1), square)
+    return wide[:, :LANES] + wide[:, LANES:]
 
 
 def front_kernel(
@@ -532,7 +537,7 @@
         ]
         + [scratch(2 * rows, LANES)] * ACCS
         + [pltpu.SemaphoreType.DMA] * 3,
-        compiler_params=params(62),
+        compiler_params=params(63),
         name="back",
     )(counts, groups, slots, pos, near, message, packed, sources, targets)
 

time: 129 us -> 127 us (0.984)
  the two profiles are of different devices: /device:TPU:79 before, /device:TPU:157 now
where the time goes in v6:
time: 127 us; the launch traced here: 126 us
  Pallas kernels  103 us (81%)
  starting transfers between devices  20.6 us (16%)
  local copies, waits for them, and re-layouts  2.02 us (2%)
    pallas_call x1, Pallas kernels, near_field(): pl.pallas_call(near_kernel, out_shape=shape(rows, LANES), in_specs=[SMEM]...  44.7 us
    pallas_call x1, Pallas kernels, front(): pl.pallas_call(front_kernel, out_shape=(shape(devices * ROW_COUNT, LANES)...  32.9 us
    pallas_call x1, Pallas kernels, back(): pl.pallas_call(back_kernel, out_shape=shape(rows, LANES), in_specs=[SMEM]...  25.1 us
    all_to_all x1, starting transfers between devices, exchange(): lax.all_to_all(blocks, AXES, split_axis=0, concat_axis=0, tiled=True)  15.3 us
    ppermute x2, starting transfers between devices, shift(): return lax.ppermute(value, AXES, pairs)  5.31 us
  transfers between devices with their start and end apart: 3, of which 0 were waited for; matrix products, arithmetic and copies ran while one was open for 0% of the time, Pallas kernels for 61%

profile of v6, /device:TPU:157, one launch (start us, length us, event | category | flops | bytes accessed | tf_op | source)
XLA Modules:
  0.0 126.2 jit_solution(7301049767651233045)
XLA Ops:
  0.0 0.9 slice.13
  0.9 1.1 copy.16
  2.0 0.0 copy-start
  2.0 3.4 %collective-permute-start = (f32[4,128]{1,0:T(4,128)S(1)}, f32[4,128]{1,0:T(4,128)S(1)}, u32[]{:S(2)}, u32[]{:S(2)}) collective-permute-start(f32[4,128]{1,0:T(4,128)S(1)} %bitcast.25), channel_id=1, source_target_pairs={{0,1},{1,2},{2,3},{3,4},{4,5},{5,6},{6,7},{7,8},{8,9},{9,10},{10,1... | collective-permute-start | bytes 6152 | tf_op jit(solution)/shard_map/ppermute | solution.py:583
  5.4 1.9 %collective-permute-start.1 = (f32[4,128]{1,0:T(4,128)S(1)}, f32[4,128]{1,0:T(4,128)S(1)}, u32[]{:S(2)}, u32[]{:S(2)}) collective-permute-start(f32[4,128]{1,0:T(4,128)S(1)} %bitcast.24), channel_id=1, source_target_pairs={{1,0},{2,1},{3,2},{4,3},{5,4},{6,5},{7,6},{8,7},{9,8},{10,9},{11,1... | collective-permute-start | bytes 6152 | tf_op jit(solution)/shard_map/ppermute | solution.py:583
  7.4 0.0 copy-done
  7.4 32.9 %front.1 = (f32[2816,128]{1,0:T(8,128)}, s32[2048]{0:T(1024)}, bf16[128,256,128]{2,1,0:T(8,128)(2,1)}) custom-call(s32[128]{0:T(128)} %classes.1, s32[128]{0:T(128)} %counts.3, f32[1,128]{1,0:T(1,128)} %constant.2.clone.signs, f32[3,256,128]{2,1,0:T(8,128)} %bitcast.13, f32[256,128]{1,0:T(8,128)} %bitcast.18, f32[316,7056]{1,0:T(8,128)} %operators.1, ...), custom_call_target="tpu_custom_call" | custom-call | tf_op jit(solution)/shard_map/front/pallas_call | solution.py:490
  40.3 0.0 collective-permute-done.before
  40.3 0.0 copy-start.1
  40.3 0.0 collective-permute-done.1.after
  40.3 0.0 copy-start.2
  40.3 15.3 %all-to-all-start = ((f32[256,11,1,128]{3,2,1,0:T(1,128)}), f32[256,11,1,128]{3,2,1,0:T(1,128)}, u32[]{:S(2)}, u32[]{:S(2)}) async-start(f32[256,11,1,128]{3,2,1,0:T(1,128)} %bitcast.16), calls=%async_computation | async-start | bytes 2883584 | tf_op jit(solution)/shard_map/all_to_all | solution.py:577
  56.2 0.0 copy-done.1
  56.3 0.0 copy-done.2
  56.3 44.7 %near_field.1.near = f32[256,128]{1,0:T(8,128)} custom-call(s32[1]{0:T(128)S(6)} %copy.17.count, f32[3,256,128]{2,1,0:T(8,128)} %bitcast.14, f32[256,128]{1,0:T(8,128)} %bitcast.19, f32[4,128]{1,0:T(4,128)} %copy-done.1, f32[4,128]{1,0:T(4,128)} %copy-done.2, s32[4096]{0:T(1024)} %all_targets.4, s32[4096]{0:T(1024)} %all_sources.4), custom_call_target="tpu_custom_call" | custom-call | tf_op jit(solution)/shard_map/near_field/pallas_call | solution.py:548
  100.9 0.0 all-to-all-done
  101.0 25.1 %back.1 = f32[256,128]{1,0:T(8,128)} custom-call(s32[128]{0:T(128)} %counts.3, s32[2048]{0:T(1024)} %get-tuple-element.11.groups, s32[8,256]{1,0:T(8,128)} %bitcast.22, f32[3,256,128]{2,1,0:T(8,128)} %bitcast.15, f32[256,128]{1,0:T(8,128)} %near_field.1.near, f32[2816,128]{1,0:T(8,128)} %bitcast.6.rows_in, bf16[128,256,128]{2,1,0:T(8,128)(2,1)} %get-tuple-element.16.packed, ...), custom_call_target="tpu_custom_call" | custom-call | tf_op jit(solution)/shard_map/back/pallas_call | solution.py:522
  (2 shorter events, 0.0 us)
Async XLA Ops:
  2.0 5.4 %copy-start = (f32[1,3,256,128]{3,2,1,0:T(8,128)}, f32[1,3,256,128]{3,2,1,0:T(8,128)S(1)}, u32[]{:S(2)}) copy-start(f32[1,3,256,128]{3,2,1,0:T(8,128)S(1)} %copy.16) | copy-start | bytes 1179652
  2.0 38.3 %collective-permute-start = (f32[4,128]{1,0:T(4,128)S(1)}, f32[4,128]{1,0:T(4,128)S(1)}, u32[]{:S(2)}, u32[]{:S(2)}) collective-permute-start(f32[4,128]{1,0:T(4,128)S(1)} %bitcast.25), channel_id=1, source_target_pairs={{0,1},{1,2},{2,3},{3,4},{4,5},{5,6},{6,7},{7,8},{8,9},{9,10},{10,1... | collective-permute-start | bytes 6152 | tf_op jit(solution)/shard_map/ppermute | solution.py:583
  5.4 34.9 %collective-permute-start.1 = (f32[4,128]{1,0:T(4,128)S(1)}, f32[4,128]{1,0:T(4,128)S(1)}, u32[]{:S(2)}, u32[]{:S(2)}) collective-permute-start(f32[4,128]{1,0:T(4,128)S(1)} %bitcast.24), channel_id=1, source_target_pairs={{1,0},{2,1},{3,2},{4,3},{5,4},{6,5},{7,6},{8,7},{9,8},{10,9},{11,1... | collective-permute-start | bytes 6152 | tf_op jit(solution)/shard_map/ppermute | solution.py:583
  40.3 16.0 %copy-start.1 = (f32[4,128]{1,0:T(4,128)}, f32[4,128]{1,0:T(4,128)S(1)}, u32[]{:S(2)}) copy-start(f32[4,128]{1,0:T(4,128)S(1)} %collective-permute-done.before) | copy-start | bytes 6148
  40.3 15.9 %copy-start.2 = (f32[4,128]{1,0:T(4,128)}, f32[4,128]{1,0:T(4,128)S(1)}, u32[]{:S(2)}) copy-start(f32[4,128]{1,0:T(4,128)S(1)} %collective-permute-done.1.after) | copy-start | bytes 6148
  40.3 60.6 %all-to-all-start = ((f32[256,11,1,128]{3,2,1,0:T(1,128)}), f32[256,11,1,128]{3,2,1,0:T(1,128)}, u32[]{:S(2)}, u32[]{:S(2)}) async-start(f32[256,11,1,128]{3,2,1,0:T(1,128)} %bitcast.16), calls=%async_computation | async-start | bytes 2883584 | tf_op jit(solution)/shard_map/all_to_all | solution.py:577
